TPU v7x, 512 devices: a whole 4x4x16 slice. The times are simulated.
512 devices in a mesh: dp: 8 (over z_lo, core), head: 64 (over z_hi, x, y).
Axes of the slice: x: 4, y: 4, z: 16 (z_hi: 4, z_lo: 4; z = z_hi * 4 + z_lo), core: 2. Of those that a mesh axis runs over, the one named last changes fastest.
Arguments:
- queries: bfloat16 [32, 2, 128, 128], P('dp', None, 'head')
- cache_keys: bfloat16 [32, 1024, 64, 128], P('dp', None, 'head'), as said below
- cache_values: bfloat16 [32, 1024, 64, 128], P('dp', None, 'head'), as said below
- new_keys: bfloat16 [32, 2, 64, 128], P('dp', None, 'head'), as said below
- new_values: bfloat16 [32, 2, 64, 128], P('dp', None, 'head'), as said below
- key_index: int32 [64, 128], P('head'), may hold values from 0 to 15, as said below
- value_index: int32 [64, 128], P('head'), may hold values from 0 to 15, as said below
- scale_table: float32 [16], replicated, may hold values from 0.25 to 2
- lengths: int32 [32], P('dp'), may hold values from 1 to 1024, as said below
- head_mix: float32 [128, 128], replicated, may hold values from -0.5 to 0.5
- channel_mix: float32 [128, 128], replicated, may hold values from -0.5 to 0.5
- out_weight: bfloat16 [16384, 16384], P('head', 'dp'), may hold values from -0.046875 to 0.046875
- residual: bfloat16 [64, 16384], P(None, ('dp', 'head')), may hold values from -6 to 6
Outputs:
- layer_out: bfloat16 [64, 16384], P(None, ('dp', 'head'))
Inputs may be any that keep to these rules, and one draw needn't show every extreme that they name: `lengths`: sequence 0 uses its whole cache. `cache_keys`: copies c and c2 are equal where c * 8 // 64 == c2 * 8 // 64. `cache_values`: copied likewise. `new_keys`: copied likewise. `new_values`: copied likewise. `key_index`: copied likewise. `value_index`: copied likewise.
All inputs are finite; a program needn't handle non-finite values.
Results may differ from a plain program's by a relative error of at most 0.0056.
The roundings to bfloat16 on the way count: a program that leaves them out, or rounds other values in their place, can miss the bound.
Values may be sent and summed in bfloat16 or wider, within the bound.
A program may use at most 64 MiB of HBM per device.

v0:
```python
import jax
import jax.numpy as jnp
from jax import lax
from jax.sharding import PartitionSpec as P


def lookup_scales(index, scale_table):
    levels = scale_table.shape[0]
    onehot = (index[..., None] == jnp.arange(levels)[None, None, :]).astype(jnp.float32)
    return jnp.einsum("kdv,v->kd", onehot, scale_table, precision=lax.Precision.HIGHEST)


def local(
    queries,
    cache_keys,
    cache_values,
    new_keys,
    new_values,
    key_index,
    value_index,
    scale_table,
    lengths,
    head_mix,
    channel_mix,
    out_weight,
    residual,
):
    seq_count, step_count, heads_here, head_size = queries.shape
    cache_len = cache_keys.shape[1]
    inverse = 1.0 / head_size**0.5
    key_scale = lookup_scales(key_index, scale_table)[0]
    value_scale = lookup_scales(value_index, scale_table)[0]
    scaled = (queries.astype(jnp.float32) * key_scale).astype(jnp.bfloat16)
    cache_score = (
        jnp.einsum(
            "bthd,bld->bthl", scaled, cache_keys[:, :, 0, :], preferred_element_type=jnp.float32
        )
        * inverse
    )
    valid = jnp.arange(cache_len)[None, :] < lengths[:, None]
    cache_score = jnp.where(valid[:, None, None, :], cache_score, -jnp.inf)
    new_score = (
        jnp.einsum(
            "bthd,bud->bthu", queries, new_keys[:, :, 0, :], preferred_element_type=jnp.float32
        )
        * inverse
    )
    causal = jnp.arange(step_count)[:, None] >= jnp.arange(step_count)[None, :]
    new_score = jnp.where(causal[None, :, None, :], new_score, -jnp.inf)
    top = jnp.maximum(jnp.max(cache_score, axis=-1), jnp.max(new_score, axis=-1))
    cache_exp = jnp.exp(cache_score - top[..., None])
    new_exp = jnp.exp(new_score - top[..., None])
    total = jnp.sum(cache_exp, axis=-1) + jnp.sum(new_exp, axis=-1)
    from_cache = (
        jnp.einsum(
            "bthl,bld->bthd",
            cache_exp.astype(jnp.bfloat16),
            cache_values[:, :, 0, :],
            preferred_element_type=jnp.float32,
        )
        * value_scale
    )
    from_new = jnp.einsum(
        "bthu,bud->bthd",
        new_exp.astype(jnp.bfloat16),
        new_values[:, :, 0, :],
        preferred_element_type=jnp.float32,
    )
    attended = (from_cache + from_new) / total[..., None]
    row_count = seq_count * step_count
    inner = jnp.einsum(
        "bthd,de->bthe", attended, channel_mix, precision=lax.Precision.HIGHEST
    ).reshape(row_count, heads_here, head_size)
    whole = lax.all_gather(inner, "head", axis=1, tiled=True)
    own_columns = lax.dynamic_slice_in_dim(
        head_mix, lax.axis_index("head") * heads_here, heads_here, 1
    )
    mixed = jnp.einsum("rgd,gh->rhd", whole, own_columns, precision=lax.Precision.HIGHEST)
    mixed_rows = mixed.reshape(row_count, heads_here * head_size).astype(jnp.bfloat16)
    partial_terms = jnp.dot(
        lax.all_gather(mixed_rows, "dp", axis=0, tiled=True),
        out_weight,
        preferred_element_type=jnp.float32,
    )
    summed = lax.psum_scatter(partial_terms, "head", scatter_dimension=1, tiled=True)
    return (residual.astype(jnp.float32) + summed).astype(jnp.bfloat16)


def solution(mesh):
    in_specs = (
        P("dp", None, "head", None),
        P("dp", None, "head", None),
        P("dp", None, "head", None),
        P("dp", None, "head", None),
        P("dp", None, "head", None),
        P("head", None),
        P("head", None),
        P(),
        P("dp"),
        P(),
        P(),
        P("head", "dp"),
        P(None, ("dp", "head")),
    )
    out_specs = P(None, ("dp", "head"))
    return jax.shard_map(local, mesh=mesh, in_specs=in_specs, out_specs=out_specs, check_vma=False)
```

profile of v0, /device:TPU:32, one launch (start us, length us, event | category | flops | bytes accessed | tf_op | source)
XLA Modules:
  0.0 703.9 jit_solution(9464584856161106009)
XLA Ops:
  6.5 0.0 copy-start
  6.5 0.0 reduce-scatter.2.cloned.1.call-start
  6.6 0.0 copy-start.9
  6.6 0.0 copy-start.10
  6.6 0.7 copy-done.9
  7.3 0.0 copy-done.10
  7.3 0.2 convolution_bitcast_fusion.1
  7.5 0.0 copy-start.11
  7.5 0.7 copy-done.11
  8.2 0.0 copy-start.5
  8.2 0.0 copy-start.7
  8.2 0.2 convolution_bitcast_fusion
  8.4 0.5 copy-done.5
  8.9 0.0 copy-start.4
  8.9 0.0 copy-start.6
  8.9 0.1 iota_compare_fusion.4
  9.0 0.0 copy-done.7
  9.0 0.6 copy-done.4
  9.6 0.2 fusion.29
  9.8 1.7 fusion.28
  11.5 0.2 fusion.11
  11.7 0.0 copy-done.6
  11.7 0.3 convolution_multiply_fusion.1
  12.1 0.0 copy-start.8
  12.1 0.7 copy-done.8
  12.7 0.0 copy-start.1
  12.8 0.2 fusion.1
  12.9 0.6 copy-done.1
  13.6 0.2 fusion.8
  13.8 0.0 copy-start.2
  13.8 230.2 %all_gather.6 = f32[8,128,128]{2,0,1:T(8,128)S(1)} all-gather(f32[8,2,128]{2,0,1:T(8,128)S(1)} %bitcast.57), channel_id=1, replica_groups=mesh['dp'=8,'head'=64] {'head'}, dimensions={1}, use_global_device_ids=true | all-gather | bytes 532480 | tf_op jit(solution)/shard_map/all_gather | solution.py:74
  244.0 0.0 copy-done.2
  244.0 0.5 fusion.3
  244.4 13.0 %all_gather.7 = bf16[64,256]{1,0:T(8,128)(2,1)S(1)} all-gather(bf16[8,256]{1,0:T(8,128)(2,1)S(1)} %bitcast.58), channel_id=1, replica_groups=mesh['dp'=8,'head'=64] {'dp'}, dimensions={0}, use_global_device_ids=true | all-gather | bytes 36864 | tf_op jit(solution)/shard_map/all_gather | solution.py:81
  257.4 0.0 copy-done
  257.4 1.5 fusion.30
  258.9 0.0 copy-start.3
  258.9 0.0 reduce-scatter.2.cloned.1.call-update
  259.0 436.8 %reduce-scatter.2.cloned.1.call-done = f32[64,32]{0,1:T(8,128)} async-done(((f32[64,2048]{0,1:T(8,128)}), f32[64,32]{0,1:T(8,128)}) %reduce-scatter.2.cloned.1.call-update) | async-done | bytes 8208 | tf_op jit(solution)/shard_map/reduce_scatter | solution.py:85
  695.8 0.0 copy-done.3
  695.8 1.3 add_convert_fusion
  (5 shorter events, 0.1 us)
Async XLA Ops:
  6.5 250.9 %copy-start = (bf16[256,2048]{1,0:T(8,128)(2,1)S(1)}, bf16[256,2048]{1,0:T(8,128)(2,1)}, u32[]{:S(2)}) copy-start(bf16[256,2048]{1,0:T(8,128)(2,1)} %param.24) | copy-start | bytes 3145732
  6.5 689.2 %reduce-scatter.2.cloned.1.call-start = ((), (), s32[]{:S(2)}) async-start(), calls=%async_computation.1 | async-start | bytes 1064960 | tf_op jit(solution)/shard_map/reduce_scatter | solution.py:85
  6.6 0.7 copy-start.9
  6.6 0.7 copy-start.10
  7.5 0.7 copy-start.11
  8.2 0.7 copy-start.5
  8.2 0.7 copy-start.7
  8.9 0.7 copy-start.4
  8.9 2.8 copy-start.6
  12.1 0.7 copy-start.8
  12.7 0.8 copy-start.1
  13.8 230.2 %copy-start.2 = (f32[128,128]{1,0:T(8,128)S(1)}, f32[128,128]{1,0:T(8,128)}, u32[]{:S(2)}) copy-start(f32[128,128]{1,0:T(8,128)} %param.22) | copy-start | bytes 196612
  258.9 436.8 %copy-start.3 = (bf16[64,32]{0,1:T(8,128)(2,1)S(1)}, bf16[64,32]{0,1:T(8,128)(2,1)}, u32[]{:S(2)}) copy-start(bf16[64,32]{0,1:T(8,128)(2,1)} %param.25) | copy-start | bytes 12292
Sparse Core Ops, SparseCore 0:
  259.1 436.6 reduce-scatter.1
where the time goes:
time: 704 us
  waiting for transfers between devices  437 us (62%)
  blocking collectives  243 us (35%)
  between operations  13.5 us (2%)
    reduce_scatter x1, waiting for transfers between devices, local(): lax.psum_scatter(partial_terms, 'head', scatter_dimension=1, tiled=True)  437 us
    all_gather x1, blocking collectives, local(): whole = lax.all_gather(inner, 'head', axis=1, tiled=True)  230 us
  transfers between devices with their start and end apart: 1, of which 1 were waited for; matrix products, arithmetic and copies ran while one was open for 0% of the time, Pallas kernels for 0%

commit v1 on v0

v1 whole, which is shorter than its diff:
```python
import functools

import jax
import jax.numpy as jnp
from jax import lax
from jax.experimental import pallas as pl
from jax.experimental.pallas import tpu as pltpu
from jax.sharding import PartitionSpec as P

MESH = pl.DeviceIdType.MESH
F32, BF16 = jnp.float32, jnp.bfloat16
DP, NZ, NP = 8, 4, 16
SEQ, STEPS, HEADS, HD, CACHE = 4, 2, 2, 128, 1024
ROWS = SEQ * STEPS
NT = (((1,), (1,)), ((), ()))


def split2(x):
    high = x.astype(BF16)
    return high, (x - high.astype(F32)).astype(BF16)


def dot(a, b):
    return jnp.dot(a, b, preferred_element_type=F32)


def dot_nt(a, b):
    return lax.dot_general(a, b, NT, preferred_element_type=F32)


def kernel(
    q_hbm, k_hbm, v_hbm, nk_hbm, nv_hbm, ki_hbm, vi_hbm, tab_hbm, len_hbm, hm_hbm, cm_hbm, w_hbm, res_hbm,
    out_ref,
    q_v, k_v, v_v, nk_v, nv_v, ki_v, vi_v, tab_s, len_s, hm_v, cm_v, w_v, res_v,
    wt, kron, z_buf, p_send, p_buf, d_send, d_buf, o_send, o_buf, f_send, f_buf,
    in_sem, k_sem, v_sem,
    z_ss, z_rs, p_ss, p_rs, d_ss, d_rs, o_ss, o_rs, f_ss, f_rs,
):
    j = lax.axis_index("dp")
    i = lax.axis_index("head")
    z = i // NP
    p = i % NP
    x = p // 4
    y = p % 4

    small = [
        (q_hbm, q_v), (ki_hbm, ki_v), (tab_hbm, tab_s), (len_hbm, len_s), (nk_hbm, nk_v), (nv_hbm, nv_v),
        (vi_hbm, vi_v), (hm_hbm, hm_v), (cm_hbm, cm_v), (res_hbm, res_v), (w_hbm, w_v),
    ]
    loads = [pltpu.make_async_copy(a, b, in_sem.at[n]) for n, (a, b) in enumerate(small)]
    k_loads = [pltpu.make_async_copy(k_hbm.at[s], k_v.at[s], k_sem.at[s]) for s in range(SEQ)]
    v_loads = [pltpu.make_async_copy(v_hbm.at[s], v_v.at[s], v_sem.at[s]) for s in range(SEQ)]
    for c in loads[:4]:
        c.start()
    for c in k_loads:
        c.start()
    for c in loads[4:-1]:
        c.start()
    for c in v_loads:
        c.start()
    loads[-1].start()

    barrier = pltpu.get_barrier_semaphore()

    def hello(device):
        pl.semaphore_signal(barrier, inc=1, device_id=device, device_id_type=MESH)

    for n in range(1, NZ):
        hello((j, (z + n) % NZ * NP + p))

    @pl.loop(1, NP)
    def _(n):
        hello((j, z * NP + (p + n) % NP))

    for n in range(1, DP):
        hello(((j + n) % DP, i))

    for c in loads[:-1]:
        c.wait()

    m_row = lax.broadcasted_iota(jnp.int32, (NP * 16, 128), 0)
    m_col = lax.broadcasted_iota(jnp.int32, (NP * 16, 128), 1)
    pick_h = (m_col == z * 32 + m_row // 8).astype(F32)
    g_row = lax.broadcasted_iota(jnp.int32, (128, NZ * 16), 0)
    g_col = lax.broadcasted_iota(jnp.int32, (128, NZ * 16), 1)
    pick_g = (g_row == g_col // 16 * 32 + p * 2 + g_col // 8 % 2).astype(F32)
    wide = lax.dot_general(pick_h, hm_v[...], NT, precision=lax.Precision.HIGHEST, preferred_element_type=F32)
    wide = jnp.dot(wide, pick_g, precision=lax.Precision.HIGHEST, preferred_element_type=F32)
    a_row = lax.broadcasted_iota(jnp.int32, (NP * 16, NZ * 16), 0)
    a_col = lax.broadcasted_iota(jnp.int32, (NP * 16, NZ * 16), 1)
    wide = jnp.where(a_row % 8 == a_col % 8, wide, 0.0)
    wide_h, wide_l = split2(wide)
    kron[:, 0:128] = jnp.concatenate([wide_h, wide_l], axis=1)
    kron[:, 128:256] = jnp.concatenate([wide_h, jnp.zeros_like(wide_h)], axis=1)
    c_h, c_l = split2(cm_v[...])
    chan = jnp.concatenate([c_h, c_l, c_h], axis=0)

    key_scale = jnp.zeros((1, HD), F32)
    value_scale = jnp.zeros((1, HD), F32)
    for n in range(16):
        key_scale = jnp.where(ki_v[...] == n, tab_s[n], key_scale)
        value_scale = jnp.where(vi_v[...] == n, tab_s[n], value_scale)
    q_all = q_v[...].astype(F32)
    q = jnp.concatenate(
        [q_all[s, t, h : h + 1, :] for h in range(HEADS) for s in range(SEQ) for t in range(STEPS)], axis=0
    )
    scaled = (q * key_scale).astype(BF16)
    q_b = q.astype(BF16)
    nk_all = nk_v[...].astype(F32)
    nv_all = nv_v[...].astype(F32)
    nk = jnp.concatenate([nk_all[s] for s in range(SEQ)], axis=0).astype(BF16)
    nv = jnp.concatenate([nv_all[s] for s in range(SEQ)], axis=0).astype(BF16)

    row = lax.broadcasted_iota(jnp.int32, (16, CACHE), 0)
    row_seq = row % 8 // 2
    score = jnp.zeros((16, CACHE), F32)
    length = jnp.zeros((16, CACHE), jnp.int32)
    for s in range(SEQ):
        k_loads[s].wait()
        score = jnp.where(row_seq == s, dot_nt(scaled, k_v[s]), score)
        length = jnp.where(row_seq == s, len_s[s], length)
    inverse = 1.0 / HD**0.5
    place = lax.broadcasted_iota(jnp.int32, (16, CACHE), 1)
    score = jnp.where(place < length, score * inverse, -jnp.inf)
    new_row = lax.broadcasted_iota(jnp.int32, (16, 8), 0)
    new_col = lax.broadcasted_iota(jnp.int32, (16, 8), 1)
    seen = (new_row % 8 // 2 == new_col // 2) & (new_col % 2 <= new_row % 2)
    new_score = jnp.where(seen, dot_nt(q_b, nk) * inverse, -jnp.inf)
    top = jnp.maximum(jnp.max(score, axis=1, keepdims=True), jnp.max(new_score, axis=1, keepdims=True))
    weight = jnp.exp(score - top)
    new_weight = jnp.exp(new_score - top)
    total = jnp.sum(weight, axis=1, keepdims=True) + jnp.sum(new_weight, axis=1, keepdims=True)
    weight = weight.astype(BF16)
    attended = jnp.zeros((16, HD), F32)
    for s in range(SEQ):
        v_loads[s].wait()
        attended = jnp.where(row_seq[:, :HD] == s, dot(weight, v_v[s]), attended)
    attended = (attended * value_scale + dot(new_weight.astype(BF16), nv)) / total
    a_h, a_l = split2(attended)
    inner = dot(jnp.concatenate([a_h, a_h, a_l], axis=1), chan)
    z_buf[z] = inner

    pl.semaphore_wait(barrier, NZ - 1 + NP - 1 + DP - 1)

    def z_copy(n):
        return pltpu.make_async_remote_copy(
            z_buf.at[z], z_buf.at[z], z_ss.at[n], z_rs.at[n], (j, (z + n) % NZ * NP + p), MESH
        )

    for n in range(1, NZ):
        z_copy(n).start()

    loads[-1].wait()

    @pl.loop(0, 16)
    def _(t):
        turned = w_v[:, pl.ds(pl.multiple_of(t * 128, 128), 128)].astype(F32).T.astype(BF16)
        for n in range(8):
            start = pl.multiple_of((t % 4 * 4 + n // 2) * 64 + t // 4 * 16, 16)
            wt[pl.ds(start, 16), n % 2 * 256 : n % 2 * 256 + 256] = turned[n * 16 : n * 16 + 16, :]

    for n in range(1, NZ):
        z_copy(n).wait_recv()

    held_h, held_l = split2(z_buf[...].reshape(NZ * 16, HD))
    held = jnp.concatenate([held_h, held_h, held_l, jnp.zeros_like(held_l)], axis=0)
    p_send[...] = dot(kron[...], held).astype(BF16).reshape(NP, 16, HD)

    def p_copy(n):
        to = (p + n) % NP
        return pltpu.make_async_remote_copy(
            p_send.at[to], p_buf.at[p], p_ss.at[n], p_rs.at[n], (j, z * NP + to), MESH
        )

    @pl.loop(1, NP)
    def _(n):
        p_copy(n).start()

    def p_take(n, total):
        p_copy(n).wait_recv()
        return total + p_buf[(p + NP - n) % NP].astype(F32)

    mixed = lax.fori_loop(1, NP, p_take, p_send[p].astype(F32))

    d_send[...] = mixed.astype(BF16)

    def d_copy(n):
        return pltpu.make_async_remote_copy(
            d_send, d_buf.at[j], d_ss.at[n], d_rs.at[n], ((j + n) % DP, i), MESH
        )

    for n in range(1, DP):
        d_copy(n).start()
    d_buf[j] = d_send[...]
    for n in range(1, DP):
        d_copy(n).wait_recv()

    d_all = d_buf[...].astype(F32)
    rows = jnp.concatenate(
        [d_all[:, h * 8 : h * 8 + 8, :].reshape(DP * ROWS, HD).astype(BF16) for h in range(HEADS)], axis=1
    )
    none = jnp.zeros_like(rows)
    both = jnp.concatenate(
        [jnp.concatenate([rows, none], axis=1), jnp.concatenate([none, rows], axis=1)], axis=0
    )

    def o_copy(n, m):
        to = (x + n) % 4 * 4 + (y + m) % 4
        return pltpu.make_async_remote_copy(
            o_send.at[to], o_buf.at[p], o_ss.at[n * 4 + m], o_rs.at[n * 4 + m], (j, z * NP + to), MESH
        )

    for n in (2, 1, 3, 0):
        column = (x + n) % 4
        part = dot_nt(wt[pl.ds(pl.multiple_of(column * 256, 256), 256), :], both)
        o_send[pl.ds(column * 4, 4)] = part.astype(BF16).reshape(4, 64, 128)
        for m in (2, 1, 3, 0):
            if n or m:
                o_copy(n, m).start()

    summed = o_send[p].astype(F32)
    for n in (2, 1, 3, 0):
        for m in (2, 1, 3, 0):
            if n or m:
                o_copy(n, m).wait_recv()
                summed = summed + o_buf[(x + 4 - n) % 4 * 4 + (y + 4 - m) % 4].astype(F32)

    f_send[...] = summed.reshape(NZ, 16, 128)

    def f_copy(n):
        to = (z + n) % NZ
        return pltpu.make_async_remote_copy(
            f_send.at[to], f_buf.at[n], f_ss.at[n], f_rs.at[n], (j, to * NP + p), MESH
        )

    for n in range(1, NZ):
        f_copy(n).start()
    result = f_send[z]
    for n in range(1, NZ):
        f_copy(n).wait_recv()
        result = result + f_buf[n]
    result = jnp.concatenate([result[:, :64], result[:, 64:]], axis=0)
    out_ref[...] = (res_v[...].astype(F32) + result).astype(BF16)

    for n in range(1, NZ):
        z_copy(n).wait_send()

    @pl.loop(1, NP)
    def _(n):
        p_copy(n).wait_send()

    for n in range(1, DP):
        d_copy(n).wait_send()
    for n in range(4):
        for m in range(4):
            if n or m:
                o_copy(n, m).wait_send()
    for n in range(1, NZ):
        f_copy(n).wait_send()


def local(
    queries, cache_keys, cache_values, new_keys, new_values, key_index, value_index, scale_table, lengths,
    head_mix, channel_mix, out_weight, residual,
):
    vmem, dma = pltpu.VMEM, pltpu.SemaphoreType.DMA
    turned = pl.pallas_call(
        kernel,
        out_shape=jax.ShapeDtypeStruct((32, 64), BF16),
        in_specs=[pl.BlockSpec(memory_space=pl.ANY)] * 13,
        out_specs=pl.BlockSpec(memory_space=pltpu.VMEM),
        scratch_shapes=[
            vmem((SEQ, STEPS, HEADS, HD), BF16),
            vmem((SEQ, CACHE, HD), BF16),
            vmem((SEQ, CACHE, HD), BF16),
            vmem((SEQ, STEPS, HD), BF16),
            vmem((SEQ, STEPS, HD), BF16),
            vmem((1, HD), jnp.int32),
            vmem((1, HD), jnp.int32),
            pltpu.SMEM((16,), F32),
            pltpu.SMEM((SEQ,), jnp.int32),
            vmem((128, 128), F32),
            vmem((128, 128), F32),
            vmem((256, 2048), BF16),
            vmem((32, 64), BF16),
            vmem((1024, 512), BF16),
            vmem((256, 256), BF16),
            vmem((NZ, 16, HD), F32),
            vmem((NP, 16, HD), BF16),
            vmem((NP, 16, HD), BF16),
            vmem((16, HD), BF16),
            vmem((DP, 16, HD), BF16),
            vmem((NP, 64, 128), BF16),
            vmem((NP, 64, 128), BF16),
            vmem((NZ, 16, 128), F32),
            vmem((NZ, 16, 128), F32),
            dma((11,)),
            dma((SEQ,)),
            dma((SEQ,)),
            dma((NZ,)), dma((NZ,)),
            dma((NP,)), dma((NP,)),
            dma((DP,)), dma((DP,)),
            dma((NP,)), dma((NP,)),
            dma((NZ,)), dma((NZ,)),
        ],
        compiler_params=pltpu.CompilerParams(
            collective_id=0, has_side_effects=True, vmem_limit_bytes=48 * 1024 * 1024
        ),
    )(
        queries,
        cache_keys.reshape(SEQ, CACHE, HD),
        cache_values.reshape(SEQ, CACHE, HD),
        new_keys.reshape(SEQ, STEPS, HD),
        new_values.reshape(SEQ, STEPS, HD),
        key_index, value_index, scale_table, lengths, head_mix, channel_mix, out_weight, residual.T,
    )
    return turned.T


def solution(mesh):
    in_specs = (
        P("dp", None, "head", None),
        P("dp", None, "head", None),
        P("dp", None, "head", None),
        P("dp", None, "head", None),
        P("dp", None, "head", None),
        P("head", None),
        P("head", None),
        P(),
        P("dp"),
        P(),
        P(),
        P("head", "dp"),
        P(None, ("dp", "head")),
    )
    out_specs = P(None, ("dp", "head"))
    return jax.shard_map(local, mesh=mesh, in_specs=in_specs, out_specs=out_specs, check_vma=False)
```

time: 704 us -> 58.3 us (0.08)
  the two profiles are of different devices: /device:TPU:32 before, /device:TPU:1 now
where the time goes in v1:
time: 58.3 us; the launch traced here: 57.8 us
  Pallas kernels  47.8 us (82%)
  local copies, waits for them, and re-layouts  10 us (17%)
    pallas_call x1, Pallas kernels, local(): pl.pallas_call(kernel, out_shape=jax.ShapeDtypeStruct((32, 64), BF16), in...  47.8 us
    unnamed x27, local copies, waits for them, and re-layouts  10 us

profile of v1, /device:TPU:1, one launch (start us, length us, event | category | flops | bytes accessed | tf_op | source)
XLA Modules:
  0.0 57.8 jit_solution(8672607738650412348)
XLA Ops:
  0.0 0.0 copy-start.5
  0.0 0.0 copy-start.9
  0.0 0.0 copy-start.10
  0.0 0.7 %copy-done.5 = bf16[64,32]{0,1:T(8,128)(2,1)S(1)} copy-done((bf16[64,32]{0,1:T(8,128)(2,1)S(1)}, bf16[64,32]{0,1:T(8,128)(2,1)}, u32[]{:S(2)}) %copy-start.5) | copy-done | bytes 4120
  0.7 0.0 copy-done.9
  0.7 0.0 copy-done.10
  0.7 0.0 copy-start
  0.7 1.2 %copy-done = bf16[4,1024,1,128]{3,1,2,0:T(8,128)(2,1)S(1)} copy-done((bf16[4,1024,1,128]{3,1,2,0:T(8,128)(2,1)S(1)}, bf16[4,1024,1,128]{3,1,2,0:T(8,128)(2,1)}, u32[]{:S(2)}) %copy-start) | copy-done | bytes 1048600
  1.9 0.0 copy-start.1
  1.9 1.2 %copy-done.1 = bf16[4,1024,1,128]{3,1,2,0:T(8,128)(2,1)S(1)} copy-done((bf16[4,1024,1,128]{3,1,2,0:T(8,128)(2,1)S(1)}, bf16[4,1024,1,128]{3,1,2,0:T(8,128)(2,1)}, u32[]{:S(2)}) %copy-start.1) | copy-done | bytes 1048600
  3.2 0.0 copy-start.2
  3.2 1.2 %copy-done.2 = bf16[256,2048]{1,0:T(8,128)(2,1)S(1)} copy-done((bf16[256,2048]{1,0:T(8,128)(2,1)S(1)}, bf16[256,2048]{1,0:T(8,128)(2,1)}, u32[]{:S(2)}) %copy-start.2) | copy-done | bytes 1048600
  4.4 0.0 copy-start.3
  4.4 0.8 %copy-done.3 = f32[128,128]{1,0:T(8,128)S(1)} copy-done((f32[128,128]{1,0:T(8,128)S(1)}, f32[128,128]{1,0:T(8,128)}, u32[]{:S(2)}) %copy-start.3) | copy-done | bytes 65560
  5.2 0.0 copy-start.4
  5.2 0.8 %copy-done.4 = f32[128,128]{1,0:T(8,128)S(1)} copy-done((f32[128,128]{1,0:T(8,128)S(1)}, f32[128,128]{1,0:T(8,128)}, u32[]{:S(2)}) %copy-start.4) | copy-done | bytes 65560
  6.1 0.0 copy-start.6
  6.1 0.7 %copy-done.6 = bf16[4,2,2,128]{3,2,1,0:T(2,128)(2,1)S(1)} copy-done((bf16[4,2,2,128]{3,2,1,0:T(2,128)(2,1)S(1)}, bf16[4,2,2,128]{3,2,1,0:T(2,128)(2,1)}, u32[]{:S(2)}) %copy-start.6) | copy-done | bytes 4120
  6.7 0.0 copy-start.7
  6.7 0.7 %copy-done.7 = bf16[4,2,1,128]{3,1,2,0:T(2,128)(2,1)S(1)} copy-done((bf16[4,2,1,128]{3,1,2,0:T(2,128)(2,1)S(1)}, bf16[4,2,1,128]{3,1,2,0:T(2,128)(2,1)}, u32[]{:S(2)}) %copy-start.7) | copy-done | bytes 2072
  7.4 0.0 copy-start.8
  7.4 0.7 %copy-done.8 = bf16[4,2,1,128]{3,1,2,0:T(2,128)(2,1)S(1)} copy-done((bf16[4,2,1,128]{3,1,2,0:T(2,128)(2,1)S(1)}, bf16[4,2,1,128]{3,1,2,0:T(2,128)(2,1)}, u32[]{:S(2)}) %copy-start.8) | copy-done | bytes 2072
  8.1 0.0 copy-start.11
  8.1 0.7 %copy-done.11 = f32[16]{0:T(128)S(1)} copy-done((f32[16]{0:T(128)S(1)}, f32[16]{0:T(128)}, u32[]{:S(2)}) %copy-start.11) | copy-done | bytes 88
  8.8 0.0 copy-start.12
  8.8 0.7 %copy-done.12 = s32[4]{0:T(128)S(1)} copy-done((s32[4]{0:T(128)S(1)}, s32[4]{0:T(128)}, u32[]{:S(2)}) %copy-start.12) | copy-done | bytes 40
  9.4 47.8 %shard_map.127 = bf16[32,64]{1,0:T(8,128)(2,1)S(1)} custom-call(bf16[4,2,2,128]{3,2,1,0:T(2,128)(2,1)S(1)} %copy-done.6, bf16[4,1024,128]{2,1,0:T(8,128)(2,1)S(1)} %bitcast.6, bf16[4,1024,128]{2,1,0:T(8,128)(2,1)S(1)} %bitcast.7, bf16[4,2,128]{2,1,0:T(2,128)(2,1)S(1)} %bitcast.10, bf16[4,2,128]{2,1,0:T(2,128)(2,1)S(1)} %bitcast.11, s32[1,128]{1,0:T(1,128)S(1)} %copy-done.9, ...), custom_call_target="tpu_custom_call" | custom-call | tf_op jit(solution)/shard_map/pallas_call | solution.py:267
  57.2 0.6 %copy.15 = bf16[64,32]{0,1:T(8,128)(2,1)} copy(bf16[64,32]{0,1:T(8,128)(2,1)S(1)} %bitcast.8) | data formatting | bytes 8192
Async XLA Ops:
  0.0 0.7 %copy-start.5 = (bf16[64,32]{0,1:T(8,128)(2,1)S(1)}, bf16[64,32]{0,1:T(8,128)(2,1)}, u32[]{:S(2)}) copy-start(bf16[64,32]{0,1:T(8,128)(2,1)} %param.25) | copy-start | bytes 12292
  0.0 0.7 %copy-start.9 = (s32[1,128]{1,0:T(1,128)S(1)}, s32[1,128]{1,0:T(1,128)}, u32[]{:S(2)}) copy-start(s32[1,128]{1,0:T(1,128)} %ki_hbm.1) | copy-start | bytes 1540
  0.0 0.7 %copy-start.10 = (s32[1,128]{1,0:T(1,128)S(1)}, s32[1,128]{1,0:T(1,128)}, u32[]{:S(2)}) copy-start(s32[1,128]{1,0:T(1,128)} %vi_hbm.1) | copy-start | bytes 1540
  0.7 1.2 %copy-start = (bf16[4,1024,1,128]{3,1,2,0:T(8,128)(2,1)S(1)}, bf16[4,1024,1,128]{3,1,2,0:T(8,128)(2,1)}, u32[]{:S(2)}) copy-start(bf16[4,1024,1,128]{3,1,2,0:T(8,128)(2,1)} %param.14) | copy-start | bytes 3145732
  1.9 1.2 %copy-start.1 = (bf16[4,1024,1,128]{3,1,2,0:T(8,128)(2,1)S(1)}, bf16[4,1024,1,128]{3,1,2,0:T(8,128)(2,1)}, u32[]{:S(2)}) copy-start(bf16[4,1024,1,128]{3,1,2,0:T(8,128)(2,1)} %param.15) | copy-start | bytes 3145732
  3.2 1.2 %copy-start.2 = (bf16[256,2048]{1,0:T(8,128)(2,1)S(1)}, bf16[256,2048]{1,0:T(8,128)(2,1)}, u32[]{:S(2)}) copy-start(bf16[256,2048]{1,0:T(8,128)(2,1)} %w_hbm.1) | copy-start | bytes 3145732
  4.4 0.8 %copy-start.3 = (f32[128,128]{1,0:T(8,128)S(1)}, f32[128,128]{1,0:T(8,128)}, u32[]{:S(2)}) copy-start(f32[128,128]{1,0:T(8,128)} %hm_hbm.1) | copy-start | bytes 196612
  5.2 0.8 %copy-start.4 = (f32[128,128]{1,0:T(8,128)S(1)}, f32[128,128]{1,0:T(8,128)}, u32[]{:S(2)}) copy-start(f32[128,128]{1,0:T(8,128)} %cm_hbm.1) | copy-start | bytes 196612
  6.1 0.7 %copy-start.6 = (bf16[4,2,2,128]{3,2,1,0:T(2,128)(2,1)S(1)}, bf16[4,2,2,128]{3,2,1,0:T(2,128)(2,1)}, u32[]{:S(2)}) copy-start(bf16[4,2,2,128]{3,2,1,0:T(2,128)(2,1)} %q_hbm.1) | copy-start | bytes 12292
  6.7 0.7 %copy-start.7 = (bf16[4,2,1,128]{3,1,2,0:T(2,128)(2,1)S(1)}, bf16[4,2,1,128]{3,1,2,0:T(2,128)(2,1)}, u32[]{:S(2)}) copy-start(bf16[4,2,1,128]{3,1,2,0:T(2,128)(2,1)} %param.16) | copy-start | bytes 6148
  7.4 0.7 %copy-start.8 = (bf16[4,2,1,128]{3,1,2,0:T(2,128)(2,1)S(1)}, bf16[4,2,1,128]{3,1,2,0:T(2,128)(2,1)}, u32[]{:S(2)}) copy-start(bf16[4,2,1,128]{3,1,2,0:T(2,128)(2,1)} %param.17) | copy-start | bytes 6148
  8.1 0.7 %copy-start.11 = (f32[16]{0:T(128)S(1)}, f32[16]{0:T(128)}, u32[]{:S(2)}) copy-start(f32[16]{0:T(128)} %tab_hbm.1) | copy-start | bytes 196
  8.8 0.7 %copy-start.12 = (s32[4]{0:T(128)S(1)}, s32[4]{0:T(128)}, u32[]{:S(2)}) copy-start(s32[4]{0:T(128)} %len_hbm.1) | copy-start | bytes 52

commit v2 on v1

--- a/solution.py
+++ b/solution.py
@@ -12,6 +12,9 @@
 DP, NZ, NP = 8, 4, 16
 SEQ, STEPS, HEADS, HD, CACHE = 4, 2, 2, 128, 1024
 ROWS = SEQ * STEPS
+FAR = [(n, m) for n in (2, 1, 3, 0) for m in (2, 1, 3, 0) if n or m]
+NEAR = sorted(FAR, key=lambda at: min(at[0], 4 - at[0]) + min(at[1], 4 - at[1]))
+SLOTS = (2, 1, 3, 0)
 NT = (((1,), (1,)), ((), ()))
 
 
@@ -43,39 +46,45 @@
     x = p // 4
     y = p % 4
 
+    barrier = pltpu.get_barrier_semaphore()
+
+    def hello(device):
+        pl.semaphore_signal(barrier, inc=1, device_id=device, device_id_type=MESH)
+
+    late = z >= 2
+    pair = z + 1 - 2 * (z % 2)
+    facing = 3 - z
+    across = (z + 2) % NZ
+    hello((j, facing * NP + p))
+    hello((j, pair * NP + p))
+
+    @pl.when(z < 2)
+    def _():
+        hello((j, across * NP + p))
+
+    for n in (2, 1, 3, 0):
+        for m in (2, 1, 3, 0):
+            if n or m:
+                hello((j, z * NP + (x + n) % 4 * 4 + (y + m) % 4))
+    for n in range(1, DP):
+        hello(((j + n) % DP, i))
+
     small = [
-        (q_hbm, q_v), (ki_hbm, ki_v), (tab_hbm, tab_s), (len_hbm, len_s), (nk_hbm, nk_v), (nv_hbm, nv_v),
-        (vi_hbm, vi_v), (hm_hbm, hm_v), (cm_hbm, cm_v), (res_hbm, res_v), (w_hbm, w_v),
+        (hm_hbm, hm_v), (cm_hbm, cm_v), (q_hbm, q_v), (ki_hbm, ki_v), (tab_hbm, tab_s), (len_hbm, len_s),
+        (nk_hbm, nk_v), (nv_hbm, nv_v), (vi_hbm, vi_v), (res_hbm, res_v), (w_hbm, w_v),
     ]
     loads = [pltpu.make_async_copy(a, b, in_sem.at[n]) for n, (a, b) in enumerate(small)]
     k_loads = [pltpu.make_async_copy(k_hbm.at[s], k_v.at[s], k_sem.at[s]) for s in range(SEQ)]
     v_loads = [pltpu.make_async_copy(v_hbm.at[s], v_v.at[s], v_sem.at[s]) for s in range(SEQ)]
-    for c in loads[:4]:
+    for c in loads[:-1]:
         c.start()
     for c in k_loads:
-        c.start()
-    for c in loads[4:-1]:
         c.start()
     for c in v_loads:
         c.start()
     loads[-1].start()
 
-    barrier = pltpu.get_barrier_semaphore()
-
-    def hello(device):
-        pl.semaphore_signal(barrier, inc=1, device_id=device, device_id_type=MESH)
-
-    for n in range(1, NZ):
-        hello((j, (z + n) % NZ * NP + p))
-
-    @pl.loop(1, NP)
-    def _(n):
-        hello((j, z * NP + (p + n) % NP))
-
-    for n in range(1, DP):
-        hello(((j + n) % DP, i))
-
-    for c in loads[:-1]:
+    for c in loads[:2]:
         c.wait()
 
     m_row = lax.broadcasted_iota(jnp.int32, (NP * 16, 128), 0)
@@ -90,11 +99,12 @@
     a_col = lax.broadcasted_iota(jnp.int32, (NP * 16, NZ * 16), 1)
     wide = jnp.where(a_row % 8 == a_col % 8, wide, 0.0)
     wide_h, wide_l = split2(wide)
-    kron[:, 0:128] = jnp.concatenate([wide_h, wide_l], axis=1)
-    kron[:, 128:256] = jnp.concatenate([wide_h, jnp.zeros_like(wide_h)], axis=1)
+    kron[...] = jnp.concatenate([wide_h, wide_l], axis=1)
     c_h, c_l = split2(cm_v[...])
     chan = jnp.concatenate([c_h, c_l, c_h], axis=0)
 
+    for c in loads[2:-1]:
+        c.wait()
     key_scale = jnp.zeros((1, HD), F32)
     value_scale = jnp.zeros((1, HD), F32)
     for n in range(16):
@@ -138,49 +148,63 @@
     attended = (attended * value_scale + dot(new_weight.astype(BF16), nv)) / total
     a_h, a_l = split2(attended)
     inner = dot(jnp.concatenate([a_h, a_h, a_l], axis=1), chan)
-    z_buf[z] = inner
-
-    pl.semaphore_wait(barrier, NZ - 1 + NP - 1 + DP - 1)
-
-    def z_copy(n):
-        return pltpu.make_async_remote_copy(
-            z_buf.at[z], z_buf.at[z], z_ss.at[n], z_rs.at[n], (j, (z + n) % NZ * NP + p), MESH
-        )
-
-    for n in range(1, NZ):
-        z_copy(n).start()
+    z_buf[z] = inner.astype(BF16)
+
+    pl.semaphore_wait(barrier, NP - 1 + DP - 1 + 2 + z // 2)
+
+    def z_copy(n, block, to):
+        return pltpu.make_async_remote_copy(
+            z_buf.at[block], z_buf.at[block], z_ss.at[n], z_rs.at[block], (j, to * NP + p), MESH
+        )
+
+    straight = z_copy(2, z, across)
+    onward = z_copy(2, pair, facing)
+
+    @pl.when(late)
+    def _():
+        straight.start()
+
+    z_copy(0, z, facing).start()
+    z_copy(1, z, pair).start()
+
+    @pl.when(z < 2)
+    def _():
+        z_copy(1, pair, pair).wait_recv()
+        onward.start()
 
     loads[-1].wait()
-
-    @pl.loop(0, 16)
-    def _(t):
-        turned = w_v[:, pl.ds(pl.multiple_of(t * 128, 128), 128)].astype(F32).T.astype(BF16)
-        for n in range(8):
-            start = pl.multiple_of((t % 4 * 4 + n // 2) * 64 + t // 4 * 16, 16)
-            wt[pl.ds(start, 16), n % 2 * 256 : n % 2 * 256 + 256] = turned[n * 16 : n * 16 + 16, :]
-
-    for n in range(1, NZ):
-        z_copy(n).wait_recv()
-
-    held_h, held_l = split2(z_buf[...].reshape(NZ * 16, HD))
-    held = jnp.concatenate([held_h, held_h, held_l, jnp.zeros_like(held_l)], axis=0)
-    p_send[...] = dot(kron[...], held).astype(BF16).reshape(NP, 16, HD)
-
-    def p_copy(n):
-        to = (p + n) % NP
-        return pltpu.make_async_remote_copy(
-            p_send.at[to], p_buf.at[p], p_ss.at[n], p_rs.at[n], (j, z * NP + to), MESH
-        )
-
-    @pl.loop(1, NP)
-    def _(n):
-        p_copy(n).start()
-
-    def p_take(n, total):
-        p_copy(n).wait_recv()
-        return total + p_buf[(p + NP - n) % NP].astype(F32)
-
-    mixed = lax.fori_loop(1, NP, p_take, p_send[p].astype(F32))
+    for k, n in enumerate(SLOTS):
+        first = (z + n) % NZ * 512
+
+        @pl.loop(0, 4)
+        def _(t, k=k, first=first):
+            turned = w_v[:, pl.ds(pl.multiple_of(first + t * 128, 128), 128)].astype(F32).T.astype(BF16)
+            for n in range(8):
+                start = pl.multiple_of(k * 256 + (t * 4 + n // 2) * 16, 16)
+                wt[pl.ds(start, 16), n % 2 * 256 : n % 2 * 256 + 256] = turned[n * 16 : n * 16 + 16, :]
+
+    @pl.when(late)
+    def _():
+        z_copy(1, pair, pair).wait_recv()
+
+    z_copy(0, facing, facing).wait_recv()
+    z_copy(2, across, across).wait_recv()
+
+    held = z_buf[...].reshape(NZ * 16, HD)
+    p_send[...] = dot(kron[...], jnp.concatenate([held, held], axis=0)).astype(BF16).reshape(NP, 16, HD)
+
+    def p_copy(n, m):
+        to = (x + n) % 4 * 4 + (y + m) % 4
+        return pltpu.make_async_remote_copy(
+            p_send.at[to], p_buf.at[p], p_ss.at[n * 4 + m], p_rs.at[n * 4 + m], (j, z * NP + to), MESH
+        )
+
+    for n, m in FAR:
+        p_copy(n, m).start()
+    mixed = p_send[p].astype(F32)
+    for n, m in NEAR:
+        p_copy(n, m).wait_recv()
+        mixed = mixed + p_buf[(x + 4 - n) % 4 * 4 + (y + 4 - m) % 4].astype(F32)
 
     d_send[...] = mixed.astype(BF16)
 
@@ -189,7 +213,7 @@
             d_send, d_buf.at[j], d_ss.at[n], d_rs.at[n], ((j + n) % DP, i), MESH
         )
 
-    for n in range(1, DP):
+    for n in (4, 3, 5, 2, 6, 1, 7):
         d_copy(n).start()
     d_buf[j] = d_send[...]
     for n in range(1, DP):
@@ -204,59 +228,61 @@
         [jnp.concatenate([rows, none], axis=1), jnp.concatenate([none, rows], axis=1)], axis=0
     )
 
-    def o_copy(n, m):
+    def o_copy(part, n, m):
         to = (x + n) % 4 * 4 + (y + m) % 4
-        return pltpu.make_async_remote_copy(
-            o_send.at[to], o_buf.at[p], o_ss.at[n * 4 + m], o_rs.at[n * 4 + m], (j, z * NP + to), MESH
-        )
-
-    for n in (2, 1, 3, 0):
-        column = (x + n) % 4
-        part = dot_nt(wt[pl.ds(pl.multiple_of(column * 256, 256), 256), :], both)
-        o_send[pl.ds(column * 4, 4)] = part.astype(BF16).reshape(4, 64, 128)
-        for m in (2, 1, 3, 0):
-            if n or m:
-                o_copy(n, m).start()
-
-    summed = o_send[p].astype(F32)
-    for n in (2, 1, 3, 0):
-        for m in (2, 1, 3, 0):
-            if n or m:
-                o_copy(n, m).wait_recv()
-                summed = summed + o_buf[(x + 4 - n) % 4 * 4 + (y + 4 - m) % 4].astype(F32)
-
-    f_send[...] = summed.reshape(NZ, 16, 128)
-
-    def f_copy(n):
-        to = (z + n) % NZ
-        return pltpu.make_async_remote_copy(
-            f_send.at[to], f_buf.at[n], f_ss.at[n], f_rs.at[n], (j, to * NP + p), MESH
-        )
-
-    for n in range(1, NZ):
-        f_copy(n).start()
-    result = f_send[z]
-    for n in range(1, NZ):
-        f_copy(n).wait_recv()
-        result = result + f_buf[n]
+        at = pl.ds(0, 1) if part == 0 else pl.ds(1, 3)
+        return pltpu.make_async_remote_copy(
+            o_send.at[to, at], o_buf.at[p, at], o_ss.at[part, n * 4 + m], o_rs.at[part, n * 4 + m], (j, z * NP + to), MESH
+        )
+
+    o_send[:, 0] = dot_nt(wt[0:256, :], both).astype(BF16).reshape(NP, 16, 128)
+    for n, m in FAR:
+        o_copy(0, n, m).start()
+    for k in range(1, NZ):
+        o_send[:, k] = dot_nt(wt[k * 256 : k * 256 + 256, :], both).astype(BF16).reshape(NP, 16, 128)
+    for n, m in FAR:
+        o_copy(1, n, m).start()
+
+    def f_copy(k):
+        to = (z + SLOTS[k]) % NZ
+        return pltpu.make_async_remote_copy(
+            f_send.at[k], f_buf.at[k], f_ss.at[k], f_rs.at[k], (j, to * NP + p), MESH
+        )
+
+    def source(n, m):
+        return (x + 4 - n) % 4 * 4 + (y + 4 - m) % 4
+
+    total = o_send[p, 0].astype(F32)
+    for n, m in NEAR:
+        o_copy(0, n, m).wait_recv()
+        total = total + o_buf[source(n, m), 0].astype(F32)
+    f_send[0] = total.astype(BF16)
+    f_copy(0).start()
+    totals = o_send[p, 1:4].astype(F32)
+    for n, m in NEAR:
+        o_copy(1, n, m).wait_recv()
+        totals = totals + o_buf[source(n, m), 1:4].astype(F32)
+    for k in (1, 2):
+        f_send[k] = totals[k - 1].astype(BF16)
+        f_copy(k).start()
+    result = totals[2]
+    for k in (1, 2, 0):
+        f_copy(k).wait_recv()
+        result = result + f_buf[k].astype(F32)
     result = jnp.concatenate([result[:, :64], result[:, 64:]], axis=0)
     out_ref[...] = (res_v[...].astype(F32) + result).astype(BF16)
 
-    for n in range(1, NZ):
-        z_copy(n).wait_send()
-
-    @pl.loop(1, NP)
-    def _(n):
-        p_copy(n).wait_send()
-
+    z_copy(0, z, facing).wait_send()
+    z_copy(1, z, pair).wait_send()
+    z_copy(2, z, across).wait_send()
     for n in range(1, DP):
         d_copy(n).wait_send()
-    for n in range(4):
-        for m in range(4):
-            if n or m:
-                o_copy(n, m).wait_send()
-    for n in range(1, NZ):
-        f_copy(n).wait_send()
+    for n, m in FAR:
+        p_copy(n, m).wait_send()
+        o_copy(0, n, m).wait_send()
+        o_copy(1, n, m).wait_send()
+    for k in range(NZ - 1):
+        f_copy(k).wait_send()
 
 
 def local(
@@ -284,27 +310,27 @@
             vmem((256, 2048), BF16),
             vmem((32, 64), BF16),
             vmem((1024, 512), BF16),
-            vmem((256, 256), BF16),
-            vmem((NZ, 16, HD), F32),
+            vmem((256, 128), BF16),
+            vmem((NZ, 16, HD), BF16),
             vmem((NP, 16, HD), BF16),
             vmem((NP, 16, HD), BF16),
             vmem((16, HD), BF16),
             vmem((DP, 16, HD), BF16),
-            vmem((NP, 64, 128), BF16),
-            vmem((NP, 64, 128), BF16),
-            vmem((NZ, 16, 128), F32),
-            vmem((NZ, 16, 128), F32),
+            vmem((NP, NZ, 16, 128), BF16),
+            vmem((NP, NZ, 16, 128), BF16),
+            vmem((NZ - 1, 16, 128), BF16),
+            vmem((NZ - 1, 16, 128), BF16),
             dma((11,)),
             dma((SEQ,)),
             dma((SEQ,)),
             dma((NZ,)), dma((NZ,)),
             dma((NP,)), dma((NP,)),
             dma((DP,)), dma((DP,)),
-            dma((NP,)), dma((NP,)),
+            dma((2, NP)), dma((2, NP)),
             dma((NZ,)), dma((NZ,)),
         ],
         compiler_params=pltpu.CompilerParams(
-            collective_id=0, has_side_effects=True, vmem_limit_bytes=48 * 1024 * 1024
+            collective_id=0, has_side_effects=True, vmem_limit_bytes=60 * 1024 * 1024
         ),
     )(
         queries,

time: 58.3 us -> 45.9 us (0.79)
  local copies, waits for them, and re-layouts: 10 us -> 1.3 us
  Pallas kernels: 47.8 us -> 43.8 us
    unnamed x27 -> x1, local copies, waits for them, and re-layouts: 10 us -> 1.3 us
    pallas_call x1, Pallas kernels: 47.8 us -> 43.8 us  [local(): pl.pallas_call(kernel, out_shape=jax.ShapeDtypeStruct((32, 64), BF16), in...]
where the time goes in v2:
time: 45.9 us; the launch traced here: 45.1 us
  Pallas kernels  43.8 us (95%)
  local copies, waits for them, and re-layouts  1.3 us (3%)
    pallas_call x1, Pallas kernels, local(): pl.pallas_call(kernel, out_shape=jax.ShapeDtypeStruct((32, 64), BF16), in...  43.8 us
    unnamed x1, local copies, waits for them, and re-layouts  1.3 us

profile of v2, /device:TPU:1, one launch (start us, length us, event | category | flops | bytes accessed | tf_op | source)
XLA Modules:
  0.0 45.1 jit_solution(17987091014622626734)
XLA Ops:
  0.0 43.8 %shard_map.127 = bf16[32,64]{1,0:T(8,128)(2,1)} custom-call(bf16[4,2,2,128]{3,2,1,0:T(2,128)(2,1)} %q_hbm.1, bf16[4,1024,128]{2,1,0:T(8,128)(2,1)} %bitcast.6, bf16[4,1024,128]{2,1,0:T(8,128)(2,1)} %bitcast.7, bf16[4,2,128]{2,1,0:T(2,128)(2,1)} %bitcast.10, bf16[4,2,128]{2,1,0:T(2,128)(2,1)} %bitcast.11, s32[1,128]{1,0:T(1,128)} %ki_hbm.1, s32[1,128]{1,0:T(1,128)} %vi_hbm.1, ...), custom_call_target="tpu_custom_call" | custom-call | tf_op jit(solution)/shard_map/pallas_call | solution.py:293
  43.8 1.3 %copy.15 = bf16[64,32]{0,1:T(8,128)(2,1)} copy(bf16[64,32]{0,1:T(8,128)(2,1)} %bitcast.8) | data formatting | bytes 8192

commit v3 on v2

--- a/solution.py
+++ b/solution.py
@@ -14,6 +14,7 @@
 ROWS = SEQ * STEPS
 FAR = [(n, m) for n in (2, 1, 3, 0) for m in (2, 1, 3, 0) if n or m]
 NEAR = sorted(FAR, key=lambda at: min(at[0], 4 - at[0]) + min(at[1], 4 - at[1]))
+FAR_Z = (8, 7, 9, 6, 10, 5, 11, 4, 12, 3, 13, 2, 14, 1, 15)
 SLOTS = (2, 1, 3, 0)
 NT = (((1,), (1,)), ((), ()))
 
@@ -35,13 +36,15 @@
     q_hbm, k_hbm, v_hbm, nk_hbm, nv_hbm, ki_hbm, vi_hbm, tab_hbm, len_hbm, hm_hbm, cm_hbm, w_hbm, res_hbm,
     out_ref,
     q_v, k_v, v_v, nk_v, nv_v, ki_v, vi_v, tab_s, len_s, hm_v, cm_v, w_v, res_v,
-    wt, kron, z_buf, p_send, p_buf, d_send, d_buf, o_send, o_buf, f_send, f_buf,
-    in_sem, k_sem, v_sem,
-    z_ss, z_rs, p_ss, p_rs, d_ss, d_rs, o_ss, o_rs, f_ss, f_rs,
+    wt, kron, a_buf, b_send, b_buf, d_buf, o_send, o_buf, f_send, f_buf,
+    in_sem, k_sem, v_sem, far_sem,
+    a_ss, a_rs, b_ss, b_rs, d_ss, d_rs, o_ss, o_rs, f_ss, f_rs,
 ):
     j = lax.axis_index("dp")
     i = lax.axis_index("head")
+    c = j % 2
     z = i // NP
+    zz = z * 4 + j // 2
     p = i % NP
     x = p // 4
     y = p % 4
@@ -51,23 +54,19 @@
     def hello(device):
         pl.semaphore_signal(barrier, inc=1, device_id=device, device_id_type=MESH)
 
-    late = z >= 2
-    pair = z + 1 - 2 * (z % 2)
-    facing = 3 - z
-    across = (z + 2) % NZ
-    hello((j, facing * NP + p))
-    hello((j, pair * NP + p))
-
-    @pl.when(z < 2)
-    def _():
-        hello((j, across * NP + p))
-
-    for n in (2, 1, 3, 0):
-        for m in (2, 1, 3, 0):
-            if n or m:
-                hello((j, z * NP + (x + n) % 4 * 4 + (y + m) % 4))
-    for n in range(1, DP):
-        hello(((j + n) % DP, i))
+    def along(n):
+        to = (zz + n) % 16
+        return to % 4 * 2 + c, to // 4 * NP + p
+
+    def plane(n, m):
+        return j, z * NP + (x + n) % 4 * 4 + (y + m) % 4
+
+    sibling = (j + 1 - 2 * c, i)
+    for n, m in FAR:
+        hello(plane(n, m))
+    for n in (4, 12, 3, 13, 2, 14, 1, 15):
+        hello(along(n))
+    hello(sibling)
 
     small = [
         (hm_hbm, hm_v), (cm_hbm, cm_v), (q_hbm, q_v), (ki_hbm, ki_v), (tab_hbm, tab_s), (len_hbm, len_s),
@@ -76,35 +75,31 @@
     loads = [pltpu.make_async_copy(a, b, in_sem.at[n]) for n, (a, b) in enumerate(small)]
     k_loads = [pltpu.make_async_copy(k_hbm.at[s], k_v.at[s], k_sem.at[s]) for s in range(SEQ)]
     v_loads = [pltpu.make_async_copy(v_hbm.at[s], v_v.at[s], v_sem.at[s]) for s in range(SEQ)]
-    for c in loads[:-1]:
-        c.start()
-    for c in k_loads:
-        c.start()
-    for c in v_loads:
-        c.start()
+    for load in loads[:-1] + k_loads + v_loads:
+        load.start()
     loads[-1].start()
 
-    for c in loads[:2]:
-        c.wait()
-
-    m_row = lax.broadcasted_iota(jnp.int32, (NP * 16, 128), 0)
-    m_col = lax.broadcasted_iota(jnp.int32, (NP * 16, 128), 1)
-    pick_h = (m_col == z * 32 + m_row // 8).astype(F32)
-    g_row = lax.broadcasted_iota(jnp.int32, (128, NZ * 16), 0)
-    g_col = lax.broadcasted_iota(jnp.int32, (128, NZ * 16), 1)
-    pick_g = (g_row == g_col // 16 * 32 + p * 2 + g_col // 8 % 2).astype(F32)
+    for load in loads[:2]:
+        load.wait()
+
+    m_row = lax.broadcasted_iota(jnp.int32, (NZ * 16, 128), 0)
+    m_col = lax.broadcasted_iota(jnp.int32, (NZ * 16, 128), 1)
+    pick_h = (m_col == m_row // 16 * 32 + p * 2 + m_row // 8 % 2).astype(F32)
+    g_row = lax.broadcasted_iota(jnp.int32, (128, NP * 16), 0)
+    g_col = lax.broadcasted_iota(jnp.int32, (128, NP * 16), 1)
+    pick_g = (g_row == z * 32 + g_col // 8).astype(F32)
     wide = lax.dot_general(pick_h, hm_v[...], NT, precision=lax.Precision.HIGHEST, preferred_element_type=F32)
     wide = jnp.dot(wide, pick_g, precision=lax.Precision.HIGHEST, preferred_element_type=F32)
-    a_row = lax.broadcasted_iota(jnp.int32, (NP * 16, NZ * 16), 0)
-    a_col = lax.broadcasted_iota(jnp.int32, (NP * 16, NZ * 16), 1)
+    a_row = lax.broadcasted_iota(jnp.int32, (NZ * 16, NP * 16), 0)
+    a_col = lax.broadcasted_iota(jnp.int32, (NZ * 16, NP * 16), 1)
     wide = jnp.where(a_row % 8 == a_col % 8, wide, 0.0)
     wide_h, wide_l = split2(wide)
     kron[...] = jnp.concatenate([wide_h, wide_l], axis=1)
     c_h, c_l = split2(cm_v[...])
     chan = jnp.concatenate([c_h, c_l, c_h], axis=0)
 
-    for c in loads[2:-1]:
-        c.wait()
+    for load in loads[2:-1]:
+        load.wait()
     key_scale = jnp.zeros((1, HD), F32)
     value_scale = jnp.zeros((1, HD), F32)
     for n in range(16):
@@ -148,29 +143,19 @@
     attended = (attended * value_scale + dot(new_weight.astype(BF16), nv)) / total
     a_h, a_l = split2(attended)
     inner = dot(jnp.concatenate([a_h, a_h, a_l], axis=1), chan)
-    z_buf[z] = inner.astype(BF16)
-
-    pl.semaphore_wait(barrier, NP - 1 + DP - 1 + 2 + z // 2)
-
-    def z_copy(n, block, to):
+    a_buf[p] = inner.astype(BF16)
+
+    pl.semaphore_wait(barrier, NP - 1 + 8 + 1)
+    for n in (4, 12):
+        pl.semaphore_signal(far_sem, inc=1, device_id=along(n), device_id_type=MESH)
+
+    def a_copy(n, m):
         return pltpu.make_async_remote_copy(
-            z_buf.at[block], z_buf.at[block], z_ss.at[n], z_rs.at[block], (j, to * NP + p), MESH
+            a_buf.at[p], a_buf.at[p], a_ss.at[n * 4 + m], a_rs.at[n * 4 + m], plane(n, m), MESH
         )
 
-    straight = z_copy(2, z, across)
-    onward = z_copy(2, pair, facing)
-
-    @pl.when(late)
-    def _():
-        straight.start()
-
-    z_copy(0, z, facing).start()
-    z_copy(1, z, pair).start()
-
-    @pl.when(z < 2)
-    def _():
-        z_copy(1, pair, pair).wait_recv()
-        onward.start()
+    for n, m in FAR:
+        a_copy(n, m).start()
 
     loads[-1].wait()
     for k, n in enumerate(SLOTS):
@@ -183,45 +168,40 @@
                 start = pl.multiple_of(k * 256 + (t * 4 + n // 2) * 16, 16)
                 wt[pl.ds(start, 16), n % 2 * 256 : n % 2 * 256 + 256] = turned[n * 16 : n * 16 + 16, :]
 
-    @pl.when(late)
-    def _():
-        z_copy(1, pair, pair).wait_recv()
-
-    z_copy(0, facing, facing).wait_recv()
-    z_copy(2, across, across).wait_recv()
-
-    held = z_buf[...].reshape(NZ * 16, HD)
-    p_send[...] = dot(kron[...], jnp.concatenate([held, held], axis=0)).astype(BF16).reshape(NP, 16, HD)
-
-    def p_copy(n, m):
-        to = (x + n) % 4 * 4 + (y + m) % 4
+    for n, m in NEAR:
+        a_copy(n, m).wait_recv()
+
+    held = a_buf[...].reshape(NP * 16, HD)
+    b_send[...] = dot(kron[...], jnp.concatenate([held, held], axis=0)).astype(BF16).reshape(NZ, 16, HD)
+    pl.semaphore_wait(far_sem, 2)
+
+    def b_copy(n):
+        to = (zz + n) % 16
         return pltpu.make_async_remote_copy(
-            p_send.at[to], p_buf.at[p], p_ss.at[n * 4 + m], p_rs.at[n * 4 + m], (j, z * NP + to), MESH
+            b_send.at[to // 4], b_buf.at[zz], b_ss.at[n], b_rs.at[n], along(n), MESH
         )
 
-    for n, m in FAR:
-        p_copy(n, m).start()
-    mixed = p_send[p].astype(F32)
-    for n, m in NEAR:
-        p_copy(n, m).wait_recv()
-        mixed = mixed + p_buf[(x + 4 - n) % 4 * 4 + (y + 4 - m) % 4].astype(F32)
-
-    d_send[...] = mixed.astype(BF16)
-
-    def d_copy(n):
-        return pltpu.make_async_remote_copy(
-            d_send, d_buf.at[j], d_ss.at[n], d_rs.at[n], ((j + n) % DP, i), MESH
-        )
-
-    for n in (4, 3, 5, 2, 6, 1, 7):
-        d_copy(n).start()
-    d_buf[j] = d_send[...]
-    for n in range(1, DP):
-        d_copy(n).wait_recv()
+    for n in FAR_Z:
+        b_copy(n).start()
+    b_buf[zz] = b_send[z]
+    for n in reversed(FAR_Z):
+        b_copy(n).wait_recv()
+    mixed = b_buf[0:4].astype(F32)
+    for n in range(1, NZ):
+        mixed = mixed + b_buf[n * 4 : n * 4 + 4].astype(F32)
+
+    d_buf[c] = mixed.astype(BF16)
+    swap = pltpu.make_async_remote_copy(d_buf.at[c], d_buf.at[c], d_ss.at[0], d_rs.at[0], sibling, MESH)
+    swap.start()
+    swap.wait_recv()
 
     d_all = d_buf[...].astype(F32)
     rows = jnp.concatenate(
-        [d_all[:, h * 8 : h * 8 + 8, :].reshape(DP * ROWS, HD).astype(BF16) for h in range(HEADS)], axis=1
+        [
+            jnp.concatenate([d_all[n % 2, n // 2, h * 8 : h * 8 + 8, :] for n in range(DP)], axis=0).astype(BF16)
+            for h in range(HEADS)
+        ],
+        axis=1,
     )
     none = jnp.zeros_like(rows)
     both = jnp.concatenate(
@@ -272,15 +252,13 @@
     result = jnp.concatenate([result[:, :64], result[:, 64:]], axis=0)
     out_ref[...] = (res_v[...].astype(F32) + result).astype(BF16)
 
-    z_copy(0, z, facing).wait_send()
-    z_copy(1, z, pair).wait_send()
-    z_copy(2, z, across).wait_send()
-    for n in range(1, DP):
-        d_copy(n).wait_send()
-    for n, m in FAR:
-        p_copy(n, m).wait_send()
+    for n, m in FAR:
+        a_copy(n, m).wait_send()
         o_copy(0, n, m).wait_send()
         o_copy(1, n, m).wait_send()
+    for n in FAR_Z:
+        b_copy(n).wait_send()
+    swap.wait_send()
     for k in range(NZ - 1):
         f_copy(k).wait_send()
 
@@ -292,7 +270,7 @@
     vmem, dma = pltpu.VMEM, pltpu.SemaphoreType.DMA
     turned = pl.pallas_call(
         kernel,
-        out_shape=jax.ShapeDtypeStruct((32, 64), BF16),
+        out_shape=pltpu.VMEM((32, 64), BF16),
         in_specs=[pl.BlockSpec(memory_space=pl.ANY)] * 13,
         out_specs=pl.BlockSpec(memory_space=pltpu.VMEM),
         scratch_shapes=[
@@ -310,12 +288,11 @@
             vmem((256, 2048), BF16),
             vmem((32, 64), BF16),
             vmem((1024, 512), BF16),
-            vmem((256, 128), BF16),
+            vmem((64, 512), BF16),
+            vmem((NP, 16, HD), BF16),
             vmem((NZ, 16, HD), BF16),
-            vmem((NP, 16, HD), BF16),
-            vmem((NP, 16, HD), BF16),
-            vmem((16, HD), BF16),
-            vmem((DP, 16, HD), BF16),
+            vmem((16, 16, HD), BF16),
+            vmem((2, NZ, 16, HD), BF16),
             vmem((NP, NZ, 16, 128), BF16),
             vmem((NP, NZ, 16, 128), BF16),
             vmem((NZ - 1, 16, 128), BF16),
@@ -323,9 +300,10 @@
             dma((11,)),
             dma((SEQ,)),
             dma((SEQ,)),
-            dma((NZ,)), dma((NZ,)),
+            pltpu.SemaphoreType.REGULAR,
             dma((NP,)), dma((NP,)),
-            dma((DP,)), dma((DP,)),
+            dma((16,)), dma((16,)),
+            dma((1,)), dma((1,)),
             dma((2, NP)), dma((2, NP)),
             dma((NZ,)), dma((NZ,)),
         ],

time: 45.9 us -> 40.6 us (0.88); the launches traced: 45.1 us -> 40.5 us
  Pallas kernels: 43.8 us -> 39.9 us
  local copies, waits for them, and re-layouts: 1.3 us -> 0.6 us
    pallas_call x1, Pallas kernels: 43.8 us -> 39.9 us  [local(): pl.pallas_call(kernel, out_shape=pltpu.VMEM((32, 64), BF16), in_specs=[pl...]
    unnamed x1, local copies, waits for them, and re-layouts: 1.3 us -> 0.6 us
where the time goes in v3:
time: 40.6 us; the launch traced here: 40.5 us
  Pallas kernels  39.9 us (98%)
  local copies, waits for them, and re-layouts  0.6 us (1%)
    pallas_call x1, Pallas kernels, local(): pl.pallas_call(kernel, out_shape=pltpu.VMEM((32, 64), BF16), in_specs=[pl...  39.9 us

profile of v3, /device:TPU:1, one launch (start us, length us, event | category | flops | bytes accessed | tf_op | source)
XLA Modules:
  0.0 40.5 jit_solution(5796311087416129881)
XLA Ops:
  0.0 39.9 %shard_map.127 = bf16[32,64]{1,0:T(8,128)(2,1)S(1)} custom-call(bf16[4,2,2,128]{3,2,1,0:T(2,128)(2,1)} %q_hbm.1, bf16[4,1024,128]{2,1,0:T(8,128)(2,1)} %bitcast.7, bf16[4,1024,128]{2,1,0:T(8,128)(2,1)} %bitcast.8, bf16[4,2,128]{2,1,0:T(2,128)(2,1)} %bitcast.10, bf16[4,2,128]{2,1,0:T(2,128)(2,1)} %bitcast.11, s32[1,128]{1,0:T(1,128)} %ki_hbm.1, ...), custom_call_target="tpu_custom_call" | custom-call | tf_op jit(solution)/shard_map/pallas_call | solution.py:271
  39.9 0.6 %copy.15 = bf16[64,32]{0,1:T(8,128)(2,1)} copy(bf16[64,32]{0,1:T(8,128)(2,1)S(1)} %bitcast.6) | data formatting | bytes 8192

commit v4 on v3

--- a/solution.py
+++ b/solution.py
@@ -15,7 +15,6 @@
 FAR = [(n, m) for n in (2, 1, 3, 0) for m in (2, 1, 3, 0) if n or m]
 NEAR = sorted(FAR, key=lambda at: min(at[0], 4 - at[0]) + min(at[1], 4 - at[1]))
 FAR_Z = (8, 7, 9, 6, 10, 5, 11, 4, 12, 3, 13, 2, 14, 1, 15)
-SLOTS = (2, 1, 3, 0)
 NT = (((1,), (1,)), ((), ()))
 
 
@@ -36,9 +35,9 @@
     q_hbm, k_hbm, v_hbm, nk_hbm, nv_hbm, ki_hbm, vi_hbm, tab_hbm, len_hbm, hm_hbm, cm_hbm, w_hbm, res_hbm,
     out_ref,
     q_v, k_v, v_v, nk_v, nv_v, ki_v, vi_v, tab_s, len_s, hm_v, cm_v, w_v, res_v,
-    wt, kron, a_buf, b_send, b_buf, d_buf, o_send, o_buf, f_send, f_buf,
+    wt, kron, a_buf, b_send, b_buf, d_buf, o_send, o_buf, e_buf, t_buf, f_send, f_buf,
     in_sem, k_sem, v_sem, far_sem,
-    a_ss, a_rs, b_ss, b_rs, d_ss, d_rs, o_ss, o_rs, f_ss, f_rs,
+    a_ss, a_rs, b_ss, b_rs, d_ss, d_rs, o_ss, o_rs, e_ss, e_rs, f_ss, f_rs,
 ):
     j = lax.axis_index("dp")
     i = lax.axis_index("head")
@@ -158,15 +157,13 @@
         a_copy(n, m).start()
 
     loads[-1].wait()
-    for k, n in enumerate(SLOTS):
-        first = (z + n) % NZ * 512
-
-        @pl.loop(0, 4)
-        def _(t, k=k, first=first):
-            turned = w_v[:, pl.ds(pl.multiple_of(first + t * 128, 128), 128)].astype(F32).T.astype(BF16)
-            for n in range(8):
-                start = pl.multiple_of(k * 256 + (t * 4 + n // 2) * 16, 16)
-                wt[pl.ds(start, 16), n % 2 * 256 : n % 2 * 256 + 256] = turned[n * 16 : n * 16 + 16, :]
+
+    @pl.loop(0, 16)
+    def _(t):
+        turned = w_v[:, pl.ds(pl.multiple_of(t * 128, 128), 128)].astype(F32).T.astype(BF16)
+        for n in range(8):
+            start = pl.multiple_of(t // 4 * 256 + (t % 4 * 4 + n // 2) * 16, 16)
+            wt[pl.ds(start, 16), n % 2 * 256 : n % 2 * 256 + 256] = turned[n * 16 : n * 16 + 16, :]
 
     for n, m in NEAR:
         a_copy(n, m).wait_recv()
@@ -215,52 +212,114 @@
             o_send.at[to, at], o_buf.at[p, at], o_ss.at[part, n * 4 + m], o_rs.at[part, n * 4 + m], (j, z * NP + to), MESH
         )
 
+    def e_copy(n, m):
+        to = (x + n) % 4 * 4 + (y + m) % 4
+        return pltpu.make_async_remote_copy(
+            o_send.at[to, 0], e_buf.at[p], e_ss.at[n * 4 + m], e_rs.at[n * 4 + m], (j, to), MESH
+        )
+
+    straight = zz == 8
     o_send[:, 0] = dot_nt(wt[0:256, :], both).astype(BF16).reshape(NP, 16, 128)
-    for n, m in FAR:
-        o_copy(0, n, m).start()
+
+    @pl.when(straight)
+    def _():
+        for n, m in FAR + [(0, 0)]:
+            e_copy(n, m).start()
+
+    @pl.when(jnp.logical_not(straight))
+    def _():
+        for n, m in FAR:
+            o_copy(0, n, m).start()
+
     for k in range(1, NZ):
         o_send[:, k] = dot_nt(wt[k * 256 : k * 256 + 256, :], both).astype(BF16).reshape(NP, 16, 128)
     for n, m in FAR:
         o_copy(1, n, m).start()
 
-    def f_copy(k):
-        to = (z + SLOTS[k]) % NZ
+    def f_copy(to):
         return pltpu.make_async_remote_copy(
-            f_send.at[k], f_buf.at[k], f_ss.at[k], f_rs.at[k], (j, to * NP + p), MESH
+            f_send.at[to], f_buf.at[z], f_ss.at[to], f_rs.at[z], (j, to * NP + p), MESH
         )
+
+    def f_wait(origin):
+        pltpu.make_async_remote_copy(
+            f_send.at[0], f_buf.at[origin], f_ss.at[0], f_rs.at[origin], (j, (z + 1) % NZ * NP + p), MESH
+        ).wait_recv()
 
     def source(n, m):
         return (x + 4 - n) % 4 * 4 + (y + 4 - m) % 4
 
-    total = o_send[p, 0].astype(F32)
-    for n, m in NEAR:
-        o_copy(0, n, m).wait_recv()
-        total = total + o_buf[source(n, m), 0].astype(F32)
-    f_send[0] = total.astype(BF16)
-    f_copy(0).start()
+    @pl.when(jnp.logical_not(straight))
+    def _():
+        total = o_send[p, 0].astype(F32)
+        for n, m in NEAR:
+            o_copy(0, n, m).wait_recv()
+            total = total + o_buf[source(n, m), 0].astype(F32)
+        t_buf[0] = total
+        f_send[0] = total.astype(BF16)
+
+        @pl.when(z > 0)
+        def _():
+            f_copy(0).start()
+
     totals = o_send[p, 1:4].astype(F32)
     for n, m in NEAR:
         o_copy(1, n, m).wait_recv()
         totals = totals + o_buf[source(n, m), 1:4].astype(F32)
-    for k in (1, 2):
-        f_send[k] = totals[k - 1].astype(BF16)
-        f_copy(k).start()
-    result = totals[2]
-    for k in (1, 2, 0):
-        f_copy(k).wait_recv()
-        result = result + f_buf[k].astype(F32)
+    t_buf[1:4] = totals
+    f_send[1:4] = totals.astype(BF16)
+    for n in (2, 1, 3):
+        to = (z + n) % NZ
+
+        @pl.when(to > 0)
+        def _(to=to):
+            f_copy(to).start()
+
+    t_buf[NZ] = t_buf[z]
+    for n in (1, 3):
+        f_wait((z + n) % NZ)
+        t_buf[NZ] += f_buf[(z + n) % NZ].astype(F32)
+
+    @pl.when(zz == 0)
+    def _():
+        extra = jnp.zeros((16, 128), F32)
+        for n, m in [(0, 0)] + NEAR:
+            e_copy(n, m).wait_recv()
+            extra = extra + e_buf[source(n, m)].astype(F32)
+        t_buf[NZ] += extra
+
+    @pl.when(zz != 0)
+    def _():
+        f_wait((z + 2) % NZ)
+        t_buf[NZ] += f_buf[(z + 2) % NZ].astype(F32)
+
+    result = t_buf[NZ]
     result = jnp.concatenate([result[:, :64], result[:, 64:]], axis=0)
     out_ref[...] = (res_v[...].astype(F32) + result).astype(BF16)
 
     for n, m in FAR:
         a_copy(n, m).wait_send()
-        o_copy(0, n, m).wait_send()
         o_copy(1, n, m).wait_send()
+
+    @pl.when(straight)
+    def _():
+        for n, m in FAR + [(0, 0)]:
+            e_copy(n, m).wait_send()
+
+    @pl.when(jnp.logical_not(straight))
+    def _():
+        for n, m in FAR:
+            o_copy(0, n, m).wait_send()
+
     for n in FAR_Z:
         b_copy(n).wait_send()
     swap.wait_send()
-    for k in range(NZ - 1):
-        f_copy(k).wait_send()
+    for to in range(NZ):
+        moved = jnp.logical_and(z != to, jnp.logical_not(straight)) if to == 0 else z != to
+
+        @pl.when(moved)
+        def _(to=to):
+            f_copy(to).wait_send()
 
 
 def local(
@@ -295,8 +354,10 @@
             vmem((2, NZ, 16, HD), BF16),
             vmem((NP, NZ, 16, 128), BF16),
             vmem((NP, NZ, 16, 128), BF16),
-            vmem((NZ - 1, 16, 128), BF16),
-            vmem((NZ - 1, 16, 128), BF16),
+            vmem((NP, 16, 128), BF16),
+            vmem((NZ + 1, 16, 128), F32),
+            vmem((NZ, 16, 128), BF16),
+            vmem((NZ, 16, 128), BF16),
             dma((11,)),
             dma((SEQ,)),
             dma((SEQ,)),
@@ -305,6 +366,7 @@
             dma((16,)), dma((16,)),
             dma((1,)), dma((1,)),
             dma((2, NP)), dma((2, NP)),
+            dma((NP,)), dma((NP,)),
             dma((NZ,)), dma((NZ,)),
         ],
         compiler_params=pltpu.CompilerParams(

time: 40.6 us -> 39.3 us (0.968)
  Pallas kernels: 39.9 us -> 38.6 us
    pallas_call x1, Pallas kernels: 39.9 us -> 38.6 us  [local(): pl.pallas_call(kernel, out_shape=pltpu.VMEM((32, 64), BF16), in_specs=[pl...]
where the time goes in v4:
time: 39.3 us; the launch traced here: 39.2 us
  Pallas kernels  38.6 us (98%)
  local copies, waits for them, and re-layouts  0.6 us (2%)
    pallas_call x1, Pallas kernels, local(): pl.pallas_call(kernel, out_shape=pltpu.VMEM((32, 64), BF16), in_specs=[pl...  38.6 us

profile of v4, /device:TPU:1, one launch (start us, length us, event | category | flops | bytes accessed | tf_op | source)
XLA Modules:
  0.0 39.2 jit_solution(17061787397343404077)
XLA Ops:
  0.0 38.6 %shard_map.127 = bf16[32,64]{1,0:T(8,128)(2,1)S(1)} custom-call(bf16[4,2,2,128]{3,2,1,0:T(2,128)(2,1)} %q_hbm.1, bf16[4,1024,128]{2,1,0:T(8,128)(2,1)} %bitcast.7, bf16[4,1024,128]{2,1,0:T(8,128)(2,1)} %bitcast.8, bf16[4,2,128]{2,1,0:T(2,128)(2,1)} %bitcast.10, bf16[4,2,128]{2,1,0:T(2,128)(2,1)} %bitcast.11, s32[1,128]{1,0:T(1,128)} %ki_hbm.1, ...), custom_call_target="tpu_custom_call" | custom-call | tf_op jit(solution)/shard_map/pallas_call | solution.py:330
  38.6 0.6 %copy.15 = bf16[64,32]{0,1:T(8,128)(2,1)} copy(bf16[64,32]{0,1:T(8,128)(2,1)S(1)} %bitcast.6) | data formatting | bytes 8192

commit v5 on v4

--- a/solution.py
+++ b/solution.py
@@ -14,6 +14,7 @@
 ROWS = SEQ * STEPS
 FAR = [(n, m) for n in (2, 1, 3, 0) for m in (2, 1, 3, 0) if n or m]
 NEAR = sorted(FAR, key=lambda at: min(at[0], 4 - at[0]) + min(at[1], 4 - at[1]))
+FIRST = (0, 1, 2, 3, 4, 8, 12, 5, 6, 7, 9, 10, 11, 13, 14, 15)
 FAR_Z = (8, 7, 9, 6, 10, 5, 11, 4, 12, 3, 13, 2, 14, 1, 15)
 NT = (((1,), (1,)), ((), ()))
 
@@ -35,7 +36,7 @@
     q_hbm, k_hbm, v_hbm, nk_hbm, nv_hbm, ki_hbm, vi_hbm, tab_hbm, len_hbm, hm_hbm, cm_hbm, w_hbm, res_hbm,
     out_ref,
     q_v, k_v, v_v, nk_v, nv_v, ki_v, vi_v, tab_s, len_s, hm_v, cm_v, w_v, res_v,
-    wt, kron, a_buf, b_send, b_buf, d_buf, o_send, o_buf, e_buf, t_buf, f_send, f_buf,
+    wt, kron, a_buf, b_send, b_buf, m_buf, o_send, o_buf, e_buf, t_buf, f_send, f_buf,
     in_sem, k_sem, v_sem, far_sem,
     a_ss, a_rs, b_ss, b_rs, d_ss, d_rs, o_ss, o_rs, e_ss, e_rs, f_ss, f_rs,
 ):
@@ -145,15 +146,16 @@
     a_buf[p] = inner.astype(BF16)
 
     pl.semaphore_wait(barrier, NP - 1 + 8 + 1)
-    for n in (4, 12):
-        pl.semaphore_signal(far_sem, inc=1, device_id=along(n), device_id_type=MESH)
-
     def a_copy(n, m):
         return pltpu.make_async_remote_copy(
             a_buf.at[p], a_buf.at[p], a_ss.at[n * 4 + m], a_rs.at[n * 4 + m], plane(n, m), MESH
         )
 
-    for n, m in FAR:
+    for n, m in FAR[:4]:
+        a_copy(n, m).start()
+    for n in (4, 12):
+        pl.semaphore_signal(far_sem, inc=1, device_id=along(n), device_id_type=MESH)
+    for n, m in FAR[4:]:
         a_copy(n, m).start()
 
     loads[-1].wait()
@@ -187,54 +189,60 @@
     for n in range(1, NZ):
         mixed = mixed + b_buf[n * 4 : n * 4 + 4].astype(F32)
 
-    d_buf[c] = mixed.astype(BF16)
-    swap = pltpu.make_async_remote_copy(d_buf.at[c], d_buf.at[c], d_ss.at[0], d_rs.at[0], sibling, MESH)
+    for h in range(HEADS):
+        m_buf[h, :, c] = mixed[:, h * 8 : h * 8 + 8, :]
+    swap = pltpu.make_async_remote_copy(m_buf.at[:, :, c], m_buf.at[:, :, c], d_ss.at[0], d_rs.at[0], sibling, MESH)
     swap.start()
     swap.wait_recv()
 
-    d_all = d_buf[...].astype(F32)
-    rows = jnp.concatenate(
-        [
-            jnp.concatenate([d_all[n % 2, n // 2, h * 8 : h * 8 + 8, :] for n in range(DP)], axis=0).astype(BF16)
-            for h in range(HEADS)
-        ],
-        axis=1,
-    )
+    rows = jnp.concatenate([m_buf[h].reshape(DP * ROWS, HD).astype(BF16) for h in range(HEADS)], axis=1)
     none = jnp.zeros_like(rows)
     both = jnp.concatenate(
         [jnp.concatenate([rows, none], axis=1), jnp.concatenate([none, rows], axis=1)], axis=0
     )
 
-    def o_copy(part, n, m):
-        to = (x + n) % 4 * 4 + (y + m) % 4
+    def o_copy(part, to, origin):
         at = pl.ds(0, 1) if part == 0 else pl.ds(1, 3)
         return pltpu.make_async_remote_copy(
-            o_send.at[to, at], o_buf.at[p, at], o_ss.at[part, n * 4 + m], o_rs.at[part, n * 4 + m], (j, z * NP + to), MESH
+            o_send.at[to, at], o_buf.at[p, at], o_ss.at[part, to], o_rs.at[part, origin], (j, z * NP + to), MESH
         )
 
-    def e_copy(n, m):
-        to = (x + n) % 4 * 4 + (y + m) % 4
-        return pltpu.make_async_remote_copy(
-            o_send.at[to, 0], e_buf.at[p], e_ss.at[n * 4 + m], e_rs.at[n * 4 + m], (j, to), MESH
-        )
-
-    straight = zz == 8
-    o_send[:, 0] = dot_nt(wt[0:256, :], both).astype(BF16).reshape(NP, 16, 128)
-
-    @pl.when(straight)
-    def _():
-        for n, m in FAR + [(0, 0)]:
-            e_copy(n, m).start()
-
-    @pl.when(jnp.logical_not(straight))
-    def _():
-        for n, m in FAR:
-            o_copy(0, n, m).start()
+    def o_wait(part, origin):
+        at = pl.ds(0, 1) if part == 0 else pl.ds(1, 3)
+        pltpu.make_async_remote_copy(
+            o_send.at[0, at], o_buf.at[origin, at], o_ss.at[part, 0], o_rs.at[part, origin], plane(1, 0), MESH
+        ).wait_recv()
+
+    def e_copy(to):
+        return pltpu.make_async_remote_copy(o_send.at[to, 0], e_buf.at[p], e_ss.at[to], e_rs.at[p], (j, to), MESH)
+
+    def e_wait(origin):
+        pltpu.make_async_remote_copy(
+            o_send.at[0, 0], e_buf.at[origin], e_ss.at[0], e_rs.at[origin], plane(1, 0), MESH
+        ).wait_recv()
+
+    straight = jnp.logical_and(z == 2, zz % 4 < 2)
+    for some, peers in (((0, 64), FIRST[:4]), ((64, 256), FIRST[4:])):
+        part = dot_nt(wt[some[0] : some[1], :], both).astype(BF16)
+        o_send[some[0] // 16 : some[1] // 16, 0] = part.reshape((some[1] - some[0]) // 16, 16, 128)
+
+        @pl.when(straight)
+        def _(peers=peers):
+            for to in peers:
+                e_copy(to).start()
+
+        @pl.when(jnp.logical_not(straight))
+        def _(peers=peers):
+            for to in peers:
+
+                @pl.when(p != to)
+                def _(to=to):
+                    o_copy(0, to, p).start()
 
     for k in range(1, NZ):
         o_send[:, k] = dot_nt(wt[k * 256 : k * 256 + 256, :], both).astype(BF16).reshape(NP, 16, 128)
     for n, m in FAR:
-        o_copy(1, n, m).start()
+        o_copy(1, (x + n) % 4 * 4 + (y + m) % 4, p).start()
 
     def f_copy(to):
         return pltpu.make_async_remote_copy(
@@ -253,7 +261,7 @@
     def _():
         total = o_send[p, 0].astype(F32)
         for n, m in NEAR:
-            o_copy(0, n, m).wait_recv()
+            o_wait(0, source(n, m))
             total = total + o_buf[source(n, m), 0].astype(F32)
         t_buf[0] = total
         f_send[0] = total.astype(BF16)
@@ -264,7 +272,7 @@
 
     totals = o_send[p, 1:4].astype(F32)
     for n, m in NEAR:
-        o_copy(1, n, m).wait_recv()
+        o_wait(1, source(n, m))
         totals = totals + o_buf[source(n, m), 1:4].astype(F32)
     t_buf[1:4] = totals
     f_send[1:4] = totals.astype(BF16)
@@ -275,20 +283,38 @@
         def _(to=to):
             f_copy(to).start()
 
+    for n, m in FAR:
+        a_copy(n, m).wait_send()
+        o_copy(1, (x + n) % 4 * 4 + (y + m) % 4, p).wait_send()
+
+    @pl.when(straight)
+    def _():
+        for to in FIRST:
+            e_copy(to).wait_send()
+
+    @pl.when(jnp.logical_not(straight))
+    def _():
+        for n, m in FAR:
+            o_copy(0, (x + n) % 4 * 4 + (y + m) % 4, p).wait_send()
+
+    for n in FAR_Z:
+        b_copy(n).wait_send()
+    swap.wait_send()
+
     t_buf[NZ] = t_buf[z]
     for n in (1, 3):
         f_wait((z + n) % NZ)
         t_buf[NZ] += f_buf[(z + n) % NZ].astype(F32)
 
-    @pl.when(zz == 0)
+    @pl.when(zz < 2)
     def _():
         extra = jnp.zeros((16, 128), F32)
         for n, m in [(0, 0)] + NEAR:
-            e_copy(n, m).wait_recv()
+            e_wait(source(n, m))
             extra = extra + e_buf[source(n, m)].astype(F32)
         t_buf[NZ] += extra
 
-    @pl.when(zz != 0)
+    @pl.when(zz >= 2)
     def _():
         f_wait((z + 2) % NZ)
         t_buf[NZ] += f_buf[(z + 2) % NZ].astype(F32)
@@ -297,23 +323,6 @@
     result = jnp.concatenate([result[:, :64], result[:, 64:]], axis=0)
     out_ref[...] = (res_v[...].astype(F32) + result).astype(BF16)
 
-    for n, m in FAR:
-        a_copy(n, m).wait_send()
-        o_copy(1, n, m).wait_send()
-
-    @pl.when(straight)
-    def _():
-        for n, m in FAR + [(0, 0)]:
-            e_copy(n, m).wait_send()
-
-    @pl.when(jnp.logical_not(straight))
-    def _():
-        for n, m in FAR:
-            o_copy(0, n, m).wait_send()
-
-    for n in FAR_Z:
-        b_copy(n).wait_send()
-    swap.wait_send()
     for to in range(NZ):
         moved = jnp.logical_and(z != to, jnp.logical_not(straight)) if to == 0 else z != to
 
@@ -351,7 +360,7 @@
             vmem((NP, 16, HD), BF16),
             vmem((NZ, 16, HD), BF16),
             vmem((16, 16, HD), BF16),
-            vmem((2, NZ, 16, HD), BF16),
+            vmem((HEADS, 4, 2, ROWS, HD), F32),
             vmem((NP, NZ, 16, 128), BF16),
             vmem((NP, NZ, 16, 128), BF16),
             vmem((NP, 16, 128), BF16),

time: 39.3 us -> 38.9 us (0.990)
  Pallas kernels: 38.6 us -> 38.2 us
where the time goes in v5:
time: 38.9 us; the launch traced here: 38.8 us
  Pallas kernels  38.2 us (98%)
  local copies, waits for them, and re-layouts  0.6 us (2%)
    pallas_call x1, Pallas kernels, local(): pl.pallas_call(kernel, out_shape=pltpu.VMEM((32, 64), BF16), in_specs=[pl...  38.2 us

profile of v5, /device:TPU:1, one launch (start us, length us, event | category | flops | bytes accessed | tf_op | source)
XLA Modules:
  0.0 38.8 jit_solution(2129710227966547226)
XLA Ops:
  0.0 38.2 %shard_map.127 = bf16[32,64]{1,0:T(8,128)(2,1)S(1)} custom-call(bf16[4,2,2,128]{3,2,1,0:T(2,128)(2,1)} %q_hbm.1, bf16[4,1024,128]{2,1,0:T(8,128)(2,1)} %bitcast.7, bf16[4,1024,128]{2,1,0:T(8,128)(2,1)} %bitcast.8, bf16[4,2,128]{2,1,0:T(2,128)(2,1)} %bitcast.10, bf16[4,2,128]{2,1,0:T(2,128)(2,1)} %bitcast.11, s32[1,128]{1,0:T(1,128)} %ki_hbm.1, ...), custom_call_target="tpu_custom_call" | custom-call | tf_op jit(solution)/shard_map/pallas_call | solution.py:339
  38.2 0.6 %copy.15 = bf16[64,32]{0,1:T(8,128)(2,1)} copy(bf16[64,32]{0,1:T(8,128)(2,1)S(1)} %bitcast.6) | data formatting | bytes 8192

commit v6 on v5

--- a/solution.py
+++ b/solution.py
@@ -37,8 +37,8 @@
     out_ref,
     q_v, k_v, v_v, nk_v, nv_v, ki_v, vi_v, tab_s, len_s, hm_v, cm_v, w_v, res_v,
     wt, kron, a_buf, b_send, b_buf, m_buf, o_send, o_buf, e_buf, t_buf, f_send, f_buf,
-    in_sem, k_sem, v_sem, far_sem,
-    a_ss, a_rs, b_ss, b_rs, d_ss, d_rs, o_ss, o_rs, e_ss, e_rs, f_ss, f_rs,
+    in_sem, k_sem, v_sem, far_sem, pair_sem,
+    a_ss, a_rs, b_ss, b_rs, g_ss, g_rs, d_ss, d_rs, o_ss, o_rs, e_ss, e_rs, f_ss, f_rs,
 ):
     j = lax.axis_index("dp")
     i = lax.axis_index("head")
@@ -177,23 +177,61 @@
     def b_copy(n):
         to = (zz + n) % 16
         return pltpu.make_async_remote_copy(
-            b_send.at[to // 4], b_buf.at[zz], b_ss.at[n], b_rs.at[n], along(n), MESH
+            b_send.at[to // 4], b_buf.at[c, zz], b_ss.at[n], b_rs.at[n], along(n), MESH
         )
+
+    def g_copy(n):
+        to = (z + n) % NZ
+        return pltpu.make_async_remote_copy(
+            b_send.at[to], b_buf.at[0, zz], g_ss.at[n], g_rs.at[zz], (1, to * NP + p), MESH
+        )
+
+    def g_wait(origin):
+        pltpu.make_async_remote_copy(
+            b_send.at[0], b_buf.at[0, origin], g_ss.at[0], g_rs.at[origin], sibling, MESH
+        ).wait_recv()
+
+    @pl.when(c == 1)
+    def _():
+        pl.semaphore_signal(pair_sem, inc=1, device_id=sibling, device_id_type=MESH)
+
+    @pl.when(c == 0)
+    def _():
+        pl.semaphore_wait(pair_sem, 1)
+        for n in (2, 1, 3, 0):
+            g_copy(n).start()
 
     for n in FAR_Z:
         b_copy(n).start()
-    b_buf[zz] = b_send[z]
+    b_buf[c, zz] = b_send[z]
     for n in reversed(FAR_Z):
         b_copy(n).wait_recv()
-    mixed = b_buf[0:4].astype(F32)
-    for n in range(1, NZ):
-        mixed = mixed + b_buf[n * 4 : n * 4 + 4].astype(F32)
-
-    for h in range(HEADS):
-        m_buf[h, :, c] = mixed[:, h * 8 : h * 8 + 8, :]
+
+    def mix(core):
+        mixed = b_buf[core, 0:4].astype(F32)
+        for n in range(1, NZ):
+            mixed = mixed + b_buf[core, n * 4 : n * 4 + 4].astype(F32)
+        for h in range(HEADS):
+            m_buf[h, :, core] = mixed[:, h * 8 : h * 8 + 8, :]
+
+    mix(c)
     swap = pltpu.make_async_remote_copy(m_buf.at[:, :, c], m_buf.at[:, :, c], d_ss.at[0], d_rs.at[0], sibling, MESH)
-    swap.start()
-    swap.wait_recv()
+    served = jnp.logical_and(zz % 4 == 0, c == 1)
+    sends = jnp.logical_or(zz % 4 != 0, c == 1)
+
+    @pl.when(sends)
+    def _():
+        swap.start()
+
+    @pl.when(jnp.logical_not(served))
+    def _():
+        swap.wait_recv()
+
+    @pl.when(served)
+    def _():
+        for n in range(16):
+            g_wait(n)
+        mix(0)
 
     rows = jnp.concatenate([m_buf[h].reshape(DP * ROWS, HD).astype(BF16) for h in range(HEADS)], axis=1)
     none = jnp.zeros_like(rows)
@@ -221,7 +259,7 @@
             o_send.at[0, 0], e_buf.at[origin], e_ss.at[0], e_rs.at[origin], plane(1, 0), MESH
         ).wait_recv()
 
-    straight = jnp.logical_and(z == 2, zz % 4 < 2)
+    straight = jnp.logical_and(z == 2, zz % 4 < 3)
     for some, peers in (((0, 64), FIRST[:4]), ((64, 256), FIRST[4:])):
         part = dot_nt(wt[some[0] : some[1], :], both).astype(BF16)
         o_send[some[0] // 16 : some[1] // 16, 0] = part.reshape((some[1] - some[0]) // 16, 16, 128)
@@ -299,14 +337,23 @@
 
     for n in FAR_Z:
         b_copy(n).wait_send()
-    swap.wait_send()
+
+    @pl.when(sends)
+    def _():
+        swap.wait_send()
+
+    @pl.when(c == 0)
+    def _():
+        for n in range(NZ):
+            g_copy(n).wait_send()
+
 
     t_buf[NZ] = t_buf[z]
     for n in (1, 3):
         f_wait((z + n) % NZ)
         t_buf[NZ] += f_buf[(z + n) % NZ].astype(F32)
 
-    @pl.when(zz < 2)
+    @pl.when(zz < 3)
     def _():
         extra = jnp.zeros((16, 128), F32)
         for n, m in [(0, 0)] + NEAR:
@@ -314,7 +361,7 @@
             extra = extra + e_buf[source(n, m)].astype(F32)
         t_buf[NZ] += extra
 
-    @pl.when(zz >= 2)
+    @pl.when(zz >= 3)
     def _():
         f_wait((z + 2) % NZ)
         t_buf[NZ] += f_buf[(z + 2) % NZ].astype(F32)
@@ -359,7 +406,7 @@
             vmem((64, 512), BF16),
             vmem((NP, 16, HD), BF16),
             vmem((NZ, 16, HD), BF16),
-            vmem((16, 16, HD), BF16),
+            vmem((2, 16, 16, HD), BF16),
             vmem((HEADS, 4, 2, ROWS, HD), F32),
             vmem((NP, NZ, 16, 128), BF16),
             vmem((NP, NZ, 16, 128), BF16),
@@ -371,8 +418,10 @@
             dma((SEQ,)),
             dma((SEQ,)),
             pltpu.SemaphoreType.REGULAR,
+            pltpu.SemaphoreType.REGULAR,
             dma((NP,)), dma((NP,)),
             dma((16,)), dma((16,)),
+            dma((NZ,)), dma((16,)),
             dma((1,)), dma((1,)),
             dma((2, NP)), dma((2, NP)),
             dma((NP,)), dma((NP,)),

time: 38.9 us -> 38 us (0.977)
  Pallas kernels: 38.2 us -> 37.1 us
    pallas_call x1, Pallas kernels: 38.2 us -> 37.1 us  [local(): pl.pallas_call(kernel, out_shape=pltpu.VMEM((32, 64), BF16), in_specs=[pl...]
where the time goes in v6:
time: 38 us; the launch traced here: 37.7 us
  Pallas kernels  37.1 us (98%)
  local copies, waits for them, and re-layouts  0.6 us (2%)
    pallas_call x1, Pallas kernels, local(): pl.pallas_call(kernel, out_shape=pltpu.VMEM((32, 64), BF16), in_specs=[pl...  37.1 us

profile of v6, /device:TPU:1, one launch (start us, length us, event | category | flops | bytes accessed | tf_op | source)
XLA Modules:
  0.0 37.7 jit_solution(6961867988247368810)
XLA Ops:
  0.0 37.1 %shard_map.127 = bf16[32,64]{1,0:T(8,128)(2,1)S(1)} custom-call(bf16[4,2,2,128]{3,2,1,0:T(2,128)(2,1)} %q_hbm.1, bf16[4,1024,128]{2,1,0:T(8,128)(2,1)} %bitcast.7, bf16[4,1024,128]{2,1,0:T(8,128)(2,1)} %bitcast.8, bf16[4,2,128]{2,1,0:T(2,128)(2,1)} %bitcast.10, bf16[4,2,128]{2,1,0:T(2,128)(2,1)} %bitcast.11, s32[1,128]{1,0:T(1,128)} %ki_hbm.1, ...), custom_call_target="tpu_custom_call" | custom-call | tf_op jit(solution)/shard_map/pallas_call | solution.py:386
  37.1 0.6 %copy.15 = bf16[64,32]{0,1:T(8,128)(2,1)} copy(bf16[64,32]{0,1:T(8,128)(2,1)S(1)} %bitcast.6) | data formatting | bytes 8192

commit v7 on v6

--- a/solution.py
+++ b/solution.py
@@ -94,7 +94,7 @@
     a_col = lax.broadcasted_iota(jnp.int32, (NZ * 16, NP * 16), 1)
     wide = jnp.where(a_row % 8 == a_col % 8, wide, 0.0)
     wide_h, wide_l = split2(wide)
-    kron[...] = jnp.concatenate([wide_h, wide_l], axis=1)
+    kron[...] = jnp.concatenate([wide_h, wide_l], axis=0)
     c_h, c_l = split2(cm_v[...])
     chan = jnp.concatenate([c_h, c_l, c_h], axis=0)
 
@@ -171,7 +171,8 @@
         a_copy(n, m).wait_recv()
 
     held = a_buf[...].reshape(NP * 16, HD)
-    b_send[...] = dot(kron[...], jnp.concatenate([held, held], axis=0)).astype(BF16).reshape(NZ, 16, HD)
+    shares = dot(kron[...], held)
+    b_send[...] = (shares[:64] + shares[64:]).astype(BF16).reshape(NZ, 16, HD)
     pl.semaphore_wait(far_sem, 2)
 
     def b_copy(n):
@@ -403,7 +404,7 @@
             vmem((256, 2048), BF16),
             vmem((32, 64), BF16),
             vmem((1024, 512), BF16),
-            vmem((64, 512), BF16),
+            vmem((128, 256), BF16),
             vmem((NP, 16, HD), BF16),
             vmem((NZ, 16, HD), BF16),
             vmem((2, 16, 16, HD), BF16),

time: 38 us -> 38 us (level)
  no operation moved by 1% of the time
where the time goes in v7:
time: 38 us; the launch traced here: 37.7 us
  Pallas kernels  37 us (97%)
  local copies, waits for them, and re-layouts  0.6 us (2%)
    pallas_call x1, Pallas kernels, local(): pl.pallas_call(kernel, out_shape=pltpu.VMEM((32, 64), BF16), in_specs=[pl...  37 us

profile of v7, /device:TPU:1, one launch (start us, length us, event | category | flops | bytes accessed | tf_op | source)
XLA Modules:
  0.0 37.7 jit_solution(2303287723689102825)
XLA Ops:
  0.0 37.0 %shard_map.127 = bf16[32,64]{1,0:T(8,128)(2,1)S(1)} custom-call(bf16[4,2,2,128]{3,2,1,0:T(2,128)(2,1)} %q_hbm.1, bf16[4,1024,128]{2,1,0:T(8,128)(2,1)} %bitcast.7, bf16[4,1024,128]{2,1,0:T(8,128)(2,1)} %bitcast.8, bf16[4,2,128]{2,1,0:T(2,128)(2,1)} %bitcast.10, bf16[4,2,128]{2,1,0:T(2,128)(2,1)} %bitcast.11, s32[1,128]{1,0:T(1,128)} %ki_hbm.1, ...), custom_call_target="tpu_custom_call" | custom-call | tf_op jit(solution)/shard_map/pallas_call | solution.py:387
  37.0 0.6 %copy.15 = bf16[64,32]{0,1:T(8,128)(2,1)} copy(bf16[64,32]{0,1:T(8,128)(2,1)S(1)} %bitcast.6) | data formatting | bytes 8192

commit v8 on v6

--- a/solution.py
+++ b/solution.py
@@ -151,11 +151,9 @@
             a_buf.at[p], a_buf.at[p], a_ss.at[n * 4 + m], a_rs.at[n * 4 + m], plane(n, m), MESH
         )
 
-    for n, m in FAR[:4]:
-        a_copy(n, m).start()
     for n in (4, 12):
         pl.semaphore_signal(far_sem, inc=1, device_id=along(n), device_id_type=MESH)
-    for n, m in FAR[4:]:
+    for n, m in FAR:
         a_copy(n, m).start()
 
     loads[-1].wait()

time: 38 us -> 38 us (level)
  no operation moved by 1% of the time
where the time goes in v8:
time: 38 us; the launch traced here: 37.7 us
  Pallas kernels  37.1 us (98%)
  local copies, waits for them, and re-layouts  0.6 us (2%)
    pallas_call x1, Pallas kernels, local(): pl.pallas_call(kernel, out_shape=pltpu.VMEM((32, 64), BF16), in_specs=[pl...  37.1 us

profile of v8, /device:TPU:1, one launch (start us, length us, event | category | flops | bytes accessed | tf_op | source)
XLA Modules:
  0.0 37.7 jit_solution(3488054476969782187)
XLA Ops:
  0.0 37.1 %shard_map.127 = bf16[32,64]{1,0:T(8,128)(2,1)S(1)} custom-call(bf16[4,2,2,128]{3,2,1,0:T(2,128)(2,1)} %q_hbm.1, bf16[4,1024,128]{2,1,0:T(8,128)(2,1)} %bitcast.7, bf16[4,1024,128]{2,1,0:T(8,128)(2,1)} %bitcast.8, bf16[4,2,128]{2,1,0:T(2,128)(2,1)} %bitcast.10, bf16[4,2,128]{2,1,0:T(2,128)(2,1)} %bitcast.11, s32[1,128]{1,0:T(1,128)} %ki_hbm.1, ...), custom_call_target="tpu_custom_call" | custom-call | tf_op jit(solution)/shard_map/pallas_call | solution.py:384
  37.1 0.6 %copy.15 = bf16[64,32]{0,1:T(8,128)(2,1)} copy(bf16[64,32]{0,1:T(8,128)(2,1)S(1)} %bitcast.6) | data formatting | bytes 8192
